TPU v7x, 256 devices: a whole 4x4x8 slice. The times are simulated.
256 devices in a mesh: ctx: 32 (over z, x_hi, core), tp: 8 (over x_lo, y).
Axes of the slice: x: 4 (x_hi: 2, x_lo: 2; x = x_hi * 2 + x_lo), y: 4, z: 8, core: 2. Of those that a mesh axis runs over, the one named last changes fastest.
Arguments:
- features: bfloat16 [3, 8192, 8192], P(None, 'ctx', 'tp'), may hold values from -6 to 6
- short_filter: bfloat16 [3, 3, 8192], P(None, None, 'tp'), may hold values from -3.5 to 3.5
- long_filter: bfloat16 [512, 128], P('tp'), may hold values from -0.5 to 0.5
- out_weight: bfloat16 [8192, 4096], P('tp'), may hold values from -0.0625 to 0.0625
- out_cotangent: bfloat16 [8192, 4096], P('ctx', 'tp'), may hold values from -6 to 6
Outputs:
- mixed: bfloat16 [8192, 4096], P('ctx', 'tp')
- feature_grads: bfloat16 [3, 8192, 8192], P(None, 'ctx', 'tp')
- filter_grad: float32 [512, 128], P('tp')
All inputs are finite; a program needn't handle non-finite values.
Results may differ from a plain program's by a relative error of at most 0.02.
Values may be sent and summed in bfloat16 or wider, within the bound.
A program may use at most 128 MiB of HBM per device.

v0:
```python
import jax
import jax.numpy as jnp
from jax import lax
from jax.sharding import PartitionSpec as P


def from_behind(block, axis, distance):
    devices = range(lax.axis_size(axis))
    route = [(i - distance, i) for i in devices if i - distance in devices]
    return lax.ppermute(block, axis, route)


def causal_short(extended, short_filter, count):
    short_taps = short_filter.shape[1]
    accumulated = jnp.zeros((extended.shape[0], count, extended.shape[2]), jnp.float32)
    for lag_index in range(short_taps):
        begin = short_taps - 1 - lag_index
        accumulated = accumulated + short_filter[:, lag_index, None, :].astype(
            jnp.float32
        ) * extended[:, begin : begin + count, :].astype(jnp.float32)
    return accumulated


def toeplitz(long_filter):
    groups, long_taps = long_filter.shape
    padded_taps = jnp.concatenate([long_filter[:, ::-1], jnp.zeros_like(long_filter)], axis=1)
    tiled = jnp.tile(padded_taps, (1, long_taps))[:, : long_taps * (2 * long_taps - 1)]
    return tiled.reshape(groups, long_taps, 2 * long_taps - 1)


def on_device(features, short_filter, long_filter, out_weight, out_cotangent):
    tok_rows = features.shape[1]
    channels = features.shape[2]
    short_taps = short_filter.shape[1]
    groups, long_taps = long_filter.shape
    group_size = channels // groups
    blocks = tok_rows // long_taps
    preceding = from_behind(features[:, tok_rows - (short_taps - 1) :], "ctx", 1)
    post = causal_short(
        jnp.concatenate([preceding, features], axis=1), short_filter, tok_rows
    ).astype(jnp.bfloat16)
    post_float = post.astype(jnp.float32)
    gated = (post_float[1] * post_float[2]).astype(jnp.bfloat16)
    carried = from_behind(gated[tok_rows - (long_taps - 1) :], "ctx", 1)
    blocked = gated.reshape(blocks, long_taps, channels)
    earlier = jnp.concatenate([carried[None], blocked[:-1, 1:]], axis=0)
    window = jnp.concatenate([earlier, blocked], axis=1).reshape(
        blocks, 2 * long_taps - 1, groups, group_size
    )
    matrix = toeplitz(long_filter)
    long_out = jnp.einsum(
        "gts,bsgc->btgc", matrix, window, preferred_element_type=jnp.float32
    ).reshape(tok_rows, channels)
    mixer = (post_float[0] * long_out).astype(jnp.bfloat16)
    partial_terms = jnp.dot(mixer, out_weight, preferred_element_type=jnp.float32)
    mixed = lax.psum_scatter(
        partial_terms.astype(jnp.bfloat16), "tp", scatter_dimension=1, tiled=True
    )
    summed = jnp.einsum(
        "tw,cw->tc",
        lax.all_gather(out_cotangent, "tp", axis=1, tiled=True),
        out_weight,
        preferred_element_type=jnp.float32,
    )
    d_mixer = summed.astype(jnp.bfloat16)
    d_mixer_float = d_mixer.astype(jnp.float32)
    d_query = d_mixer_float * long_out
    d_long = (d_mixer_float * post_float[0]).astype(jnp.bfloat16)
    d_blocks = d_long.reshape(blocks, long_taps, groups, group_size)
    correlation = jnp.einsum("btgc,bsgc->gts", d_blocks, window, preferred_element_type=jnp.float32)
    flattened = jnp.pad(
        correlation.reshape(groups, long_taps * (2 * long_taps - 1)), ((0, 0), (0, long_taps))
    )
    diagonals = flattened.reshape(groups, long_taps, 2 * long_taps).sum(axis=1)[:, :long_taps][
        :, ::-1
    ]
    norm_factor = (tok_rows * lax.axis_size("ctx") * group_size) ** (-0.5)
    filter_grad = lax.psum(diagonals, "ctx") * norm_factor
    spread = jnp.einsum(
        "gts,btgc->bsgc", matrix, d_blocks, preferred_element_type=jnp.float32
    ).reshape(blocks, 2 * long_taps - 1, channels)
    returned = from_behind(spread[0, : long_taps - 1].astype(jnp.bfloat16), "ctx", -1).astype(
        jnp.float32
    )
    following = jnp.concatenate([spread[1:, : long_taps - 1], returned[None]], axis=0)
    d_gated = (spread[:, long_taps - 1 :] + jnp.pad(following, ((0, 0), (1, 0), (0, 0)))).reshape(
        tok_rows, channels
    )
    d_post = jnp.stack([d_query, d_gated * post_float[2], d_gated * post_float[1]])
    following_rows = from_behind(d_post[:, : short_taps - 1], "ctx", -1)
    extended = jnp.concatenate([d_post, following_rows], axis=1)
    accumulated = jnp.zeros(d_post.shape, jnp.float32)
    for lag_index in range(short_taps):
        accumulated = (
            accumulated
            + short_filter[:, lag_index, None, :].astype(jnp.float32)
            * extended[:, lag_index : lag_index + tok_rows, :]
        )
    feature_grads = accumulated.astype(jnp.bfloat16)
    return (mixed, feature_grads, filter_grad)


def solution(mesh):
    placed = (
        P(None, "ctx", "tp"),
        P(None, None, "tp"),
        P("tp", None),
        P("tp", None),
        P("ctx", "tp"),
    )
    return jax.shard_map(
        on_device,
        mesh=mesh,
        in_specs=placed,
        out_specs=(P("ctx", "tp"), P(None, "ctx", "tp"), P("tp", None)),
        check_vma=False,
    )
```

profile of v0, /device:TPU:1, one launch (start us, length us, event | category | flops | bytes accessed | tf_op | source)
XLA Modules:
  0.0 271.0 jit_solution(14230718254306764930)
XLA Ops:
  7.2 0.0 all-gather.2.cloned.1.call-start
  7.2 0.7 all-gather.2.cloned.1.call-update
  7.9 0.0 reduce-scatter.2.cloned.1.call-start
  7.9 0.8 slice.69
  8.8 6.0 %collective-permute-start = (bf16[3,2,1024]{2,1,0:T(2,128)(2,1)S(1)}, bf16[3,2,1024]{2,1,0:T(2,128)(2,1)S(1)}, u32[]{:S(2)}, u32[]{:S(2)}) collective-permute-start(bf16[3,2,1024]{2,1,0:T(2,128)(2,1)S(1)} %slice.69), channel_id=1, source_target_pairs={{0,8},{8,16},{16,24},{24,32},{32,40},{40,48},{48,56},{56,64},{64,7... | collective-permute-start | bytes 36872 | tf_op jit(solution)/shard_map/ppermute | solution.py:10
  14.8 0.9 slice_convert_fusion.3
  15.7 0.8 rev.6
  16.5 0.3 tile.4
  16.8 2.6 copy.30
  19.4 2.2 slice.94
  21.7 15.8 %reshape.63 = bf16[64,128,255,1]{2,1,0,3:T(8,128)(2,1)} reshape(bf16[64,32640]{1,0:T(8,128)(2,1)} %slice.94) | data formatting | bytes 8355840 | tf_op jit(solution)/shard_map/reshape | solution.py:28
  37.5 0.0 collective-permute-done
  37.5 4.0 %fusion.11 = f32[3,256,1024]{2,1,0:T(8,128)S(1)} fusion(bf16[3,256,1024]{2,1,0:T(8,128)(2,1)} %param.5, bf16[3,2,1024]{2,1,0:T(2,128)(2,1)S(1)} %collective-permute-done, f32[3,1024]{1,0:T(4,128)S(1)} %get-tuple-element.11, f32[3,1024]{1,0:T(4,128)S(1)} %get-tuple-element.12, f32[3,1024]{1,0:T(4,128)S(1)} %bitcast.80), kind=kLoop, calls=%fused_computation.19 | loop fusion | flops 12582912 | bytes 4767744 | tf_op jit(solution)/shard_map/convert_element_type | solution.py:42
  41.5 0.0 copy-start
  41.5 11.0 %all-gather.2.cloned.1.call-done = bf16[256,4096]{1,0:T(8,128)(2,1)} async-done(((bf16[256,512]{1,0:T(8,128)(2,1)}), bf16[256,4096]{1,0:T(8,128)(2,1)}) %all-gather.2.cloned.1.call-update) | async-done | bytes 2097168 | tf_op jit(solution)/shard_map/all_gather | solution.py:61
  52.5 7.3 %fusion.16 = (bf16[256,1024]{1,0:T(8,128)(2,1)}, bf16[256,1024]{1,0:T(8,128)(2,1)}) fusion(f32[3,256,1024]{2,1,0:T(8,128)S(1)} %fusion.11, bf16[256,4096]{1,0:T(8,128)(2,1)} %all-gather.2.cloned.1.call-done, bf16[1024,4096]{1,0:T(8,128)(2,1)} %param.8), kind=kOutput, calls=%fused_computation.26 | convolution fusion | flops 2148532224 | bytes 12582912 | tf_op jit(solution)/shard_map/tw,cw->tc/dot_general | solution.py:59
  59.8 0.0 copy-done
  59.8 1.2 copy.19
  61.1 0.1 reshape.54
  61.2 0.0 copy-start.3
  61.2 3.1 %fusion.7 = f32[2,255,64,16]{1,3,0,2:T(8,128)S(1)} fusion(bf16[64,128,255,1]{2,1,0,3:T(8,128)(2,1)} %reshape.63, bf16[2,128,64,16]{1,0,3,2:T(2,128)(2,1)S(1)} %reshape.54), kind=kOutput, calls=%fused_computation.15 | convolution fusion | flops 133693440 | bytes 6791168 | tf_op jit(solution)/shard_map/gts,btgc->bsgc/dot_general | solution.py:79
  64.3 0.0 copy-done.3
  64.3 0.2 copy.21
  64.5 8.2 %collective-permute-start.2 = (bf16[127,1024]{0,1:T(8,128)(2,1)S(1)}, bf16[127,1024]{0,1:T(8,128)(2,1)S(1)}, u32[]{:S(2)}, u32[]{:S(2)}) collective-permute-start(bf16[127,1024]{0,1:T(8,128)(2,1)S(1)} %fusion.20), channel_id=1, source_target_pairs={{8,0},{16,8},{24,16},{32,24},{40,32},{48,40},{56,48},{64,56},{72,6... | collective-permute-start | bytes 780296 | tf_op jit(solution)/shard_map/ppermute | solution.py:10
  72.8 6.1 %collective-permute-done.2 = bf16[127,1024]{0,1:T(8,128)(2,1)S(1)} collective-permute-done((bf16[127,1024]{0,1:T(8,128)(2,1)S(1)}, bf16[127,1024]{0,1:T(8,128)(2,1)S(1)}, u32[]{:S(2)}, u32[]{:S(2)}) %collective-permute-start.2) | collective-permute-done | bytes 260128 | tf_op jit(solution)/shard_map/ppermute | solution.py:10
  78.9 0.6 fusion.17
  79.5 1.3 copy.22
  80.8 2.2 bitcast_multiply_fusion.1
  83.0 0.8 slice_bitcast_fusion.1
  83.8 1.9 collective-permute-start.1
  85.7 0.2 copy.14
  86.0 0.8 slice.93
  86.7 1.1 copy.29
  87.9 0.9 convert_element_type.67
  88.8 1.1 copy.15
  89.9 0.0 copy-start.1
  89.9 0.0 collective-permute-done.1
  89.9 1.3 copy.12
  91.2 0.0 copy-start.6
  91.3 3.8 %fusion.12 = f32[2,128,64,16]{1,3,0,2:T(8,128)S(1)} fusion(bf16[64,128,255,1]{2,1,0,3:T(8,128)(2,1)} %reshape.63, bf16[2,128,64,16]{1,3,0,2:T(8,128)(2,1)S(1)} %copy.15, bf16[1,127,64,16]{1,3,0,2:T(8,128)(2,1)S(1)} %bitcast.76, bf16[1,127,64,16]{1,3,0,2:T(8,128)(2,1)S(1)} %bitcast.78), kind=kOutput, calls=%fused_computation.21 | convolution fusion | flops 136826880 | bytes 6270976 | tf_op jit(solution)/shard_map/gts,bsgc->btgc/dot_general | solution.py:51
  95.1 0.0 copy-done.6
  95.1 0.5 copy.16
  95.6 1.0 copy.41
  96.7 1.6 copy.17
  98.2 0.0 copy-start.5
  98.2 7.7 %convolution_convert_fusion = bf16[256,4096]{1,0:T(8,128)(2,1)} fusion(bf16[1024,4096]{1,0:T(8,128)(2,1)} %param.8, f32[256,1024]{1,0:T(8,128)S(1)} %copy.17, f32[3,256,1024]{2,1,0:T(8,128)} %copy-done), kind=kOutput, calls=%fused_computation.1 | convolution fusion | flops 2149056512 | bytes 12582912 | tf_op jit(solution)/shard_map/dot_general | solution.py:55
  106.0 0.0 reduce-scatter.2.cloned.1.call-update
  106.0 1.5 fusion.15
  107.5 0.2 pad_maximum_fusion.1
  107.8 3.5 %collective-permute-start.3 = (f32[3,2,1024]{2,1,0:T(2,128)S(1)}, f32[3,2,1024]{2,1,0:T(2,128)S(1)}, u32[]{:S(2)}, u32[]{:S(2)}) collective-permute-start(f32[3,2,1024]{2,1,0:T(2,128)S(1)} %slice.98), channel_id=1, source_target_pairs={{8,0},{16,8},{24,16},{32,24},{40,32},{48,40},{56,48},{64,56},{72,6... | collective-permute-start | bytes 73736 | tf_op jit(solution)/shard_map/ppermute | solution.py:10
  111.3 0.0 copy-done.2
  111.3 0.0 copy-done.4
  111.3 0.0 copy-done.7
  111.3 4.6 %convolution_bitcast_fusion = f32[64,128,255]{2,1,0:T(8,128)} fusion(bf16[2,128,64,16]{1,0,3,2:T(2,128)(2,1)S(1)} %copy-done.4, bf16[2,128,64,16]{1,3,0,2:T(8,128)(2,1)S(1)} %copy-done.2, bf16[1,127,64,16]{1,3,0,2:T(8,128)(2,1)S(1)} %bitcast.77, bf16[1,127,64,16]{1,3,0,2:T(8,128)(2,1)S(1)} %bitcast.79), kind=kOutput, calls=%fused_computation.7 | convolution fusion | flops 136826880 | bytes 9924608 | tf_op jit(solution)/shard_map/btgc,bsgc->gts/dot_general | solution.py:70
  115.9 9.2 %reshape.57 = f32[64,32640]{1,0:T(8,128)} reshape(f32[64,128,255]{2,1,0:T(8,128)} %convolution_bitcast_fusion) | data formatting | bytes 16711680 | tf_op jit(solution)/shard_map/reshape | solution.py:72
  125.1 4.1 %pad.10 = f32[64,32768]{1,0:T(8,128)S(1)} pad(f32[64,32640]{1,0:T(8,128)} %reshape.57, f32[]{:T(128)} %constant.1.clone.1), padding=0_0x0_128 | pad | bytes 16744452 | tf_op jit(solution)/shard_map/jit(_pad)/pad | solution.py:71
  129.2 2.5 copy.32
  131.7 1.5 bitcast_reduce_fusion
  133.2 0.1 rev.7
  133.3 127.8 %psum.7 = f32[64,128]{1,0:T(8,128)S(1)} all-reduce(f32[64,128]{1,0:T(8,128)S(1)} %rev.7), channel_id=1, replica_groups=mesh['ctx'=32,'tp'=8] {'ctx'}, use_global_device_ids=true, to_apply=%region_2.3 | all-reduce | flops 8192 | bytes 65536 | tf_op jit(solution)/shard_map/psum | solution.py:78
  261.1 0.6 broadcast_multiply_fusion
  261.7 0.0 collective-permute-done.3
  261.7 0.2 pad_maximum_fusion
  262.0 2.2 fusion.5
  (14 shorter events, 0.2 us)
Async XLA Ops:
  7.2 45.3 %all-gather.2.cloned.1.call-start = ((), (), s32[]{:S(2)}) async-start(), calls=%async_computation.2 | async-start | bytes 2359296 | tf_op jit(solution)/shard_map/all_gather | solution.py:61
  7.9 256.2 %reduce-scatter.2.cloned.1.call-start = ((), (), s32[]{:S(2)}) async-start(), calls=%async_computation.1 | async-start | bytes 2359296 | tf_op jit(solution)/shard_map/reduce_scatter | solution.py:56
  8.8 28.7 %collective-permute-start = (bf16[3,2,1024]{2,1,0:T(2,128)(2,1)S(1)}, bf16[3,2,1024]{2,1,0:T(2,128)(2,1)S(1)}, u32[]{:S(2)}, u32[]{:S(2)}) collective-permute-start(bf16[3,2,1024]{2,1,0:T(2,128)(2,1)S(1)} %slice.69), channel_id=1, source_target_pairs={{0,8},{8,16},{16,24},{24,32},{32,40},{40,48},{48,56},{56,64},{64,7... | collective-permute-start | bytes 36872 | tf_op jit(solution)/shard_map/ppermute | solution.py:10
  41.5 18.3 %copy-start = (f32[3,256,1024]{2,1,0:T(8,128)}, f32[3,256,1024]{2,1,0:T(8,128)S(1)}, u32[]{:S(2)}) copy-start(f32[3,256,1024]{2,1,0:T(8,128)S(1)} %fusion.11) | copy-start | bytes 9437188
  61.2 3.1 %copy-start.3 = (bf16[2,128,64,16]{1,0,3,2:T(2,128)(2,1)}, bf16[2,128,64,16]{1,0,3,2:T(2,128)(2,1)S(1)}, u32[]{:S(2)}) copy-start(bf16[2,128,64,16]{1,0,3,2:T(2,128)(2,1)S(1)} %reshape.54) | copy-start | bytes 1572868
  64.5 14.4 %collective-permute-start.2 = (bf16[127,1024]{0,1:T(8,128)(2,1)S(1)}, bf16[127,1024]{0,1:T(8,128)(2,1)S(1)}, u32[]{:S(2)}, u32[]{:S(2)}) collective-permute-start(bf16[127,1024]{0,1:T(8,128)(2,1)S(1)} %fusion.20), channel_id=1, source_target_pairs={{8,0},{16,8},{24,16},{32,24},{40,32},{48,40},{56,48},{64,56},{72,6... | collective-permute-start | bytes 780296 | tf_op jit(solution)/shard_map/ppermute | solution.py:10
  83.8 6.1 %collective-permute-start.1 = (bf16[127,1024]{1,0:T(8,128)(2,1)}, bf16[127,1024]{1,0:T(8,128)(2,1)}, u32[]{:S(2)}, u32[]{:S(2)}) collective-permute-start(bf16[127,1024]{1,0:T(8,128)(2,1)} %slice_bitcast_fusion.1), channel_id=1, source_target_pairs={{0,8},{8,16},{16,24},{24,32},{32,40},{40,48},{48,56},{56,64},{64,7... | collective-permute-start | bytes 780296 | tf_op jit(solution)/shard_map/ppermute | solution.py:10
  89.9 5.2 %copy-start.1 = (bf16[2,128,64,16]{1,3,0,2:T(8,128)(2,1)}, bf16[2,128,64,16]{1,3,0,2:T(8,128)(2,1)S(1)}, u32[]{:S(2)}) copy-start(bf16[2,128,64,16]{1,3,0,2:T(8,128)(2,1)S(1)} %copy.15) | copy-start | bytes 1572868
  91.2 3.8 %copy-start.6 = (bf16[127,1024]{0,1:T(8,128)(2,1)}, bf16[127,1024]{0,1:T(8,128)(2,1)S(1)}, u32[]{:S(2)}) copy-start(bf16[127,1024]{0,1:T(8,128)(2,1)S(1)} %copy.12) | copy-start | bytes 780292
  98.2 7.8 %copy-start.5 = (f32[256,1024]{1,0:T(8,128)}, f32[256,1024]{1,0:T(8,128)S(1)}, u32[]{:S(2)}) copy-start(f32[256,1024]{1,0:T(8,128)S(1)} %copy.17) | copy-start | bytes 3145732
  107.5 3.8 %copy-start.2 = (bf16[2,128,64,16]{1,3,0,2:T(8,128)(2,1)S(1)}, bf16[2,128,64,16]{1,3,0,2:T(8,128)(2,1)}, u32[]{:S(2)}) copy-start(bf16[2,128,64,16]{1,3,0,2:T(8,128)(2,1)} %copy-done.1) | copy-start | bytes 1572868
  107.5 3.8 %copy-start.4 = (bf16[2,128,64,16]{1,0,3,2:T(2,128)(2,1)S(1)}, bf16[2,128,64,16]{1,0,3,2:T(2,128)(2,1)}, u32[]{:S(2)}) copy-start(bf16[2,128,64,16]{1,0,3,2:T(2,128)(2,1)} %copy-done.3) | copy-start | bytes 1572868
  107.5 3.8 %copy-start.7 = (bf16[127,1024]{0,1:T(8,128)(2,1)S(1)}, bf16[127,1024]{0,1:T(8,128)(2,1)}, u32[]{:S(2)}) copy-start(bf16[127,1024]{0,1:T(8,128)(2,1)} %copy-done.6) | copy-start | bytes 780292
  107.8 153.9 %collective-permute-start.3 = (f32[3,2,1024]{2,1,0:T(2,128)S(1)}, f32[3,2,1024]{2,1,0:T(2,128)S(1)}, u32[]{:S(2)}, u32[]{:S(2)}) collective-permute-start(f32[3,2,1024]{2,1,0:T(2,128)S(1)} %slice.98), channel_id=1, source_target_pairs={{8,0},{16,8},{24,16},{32,24},{40,32},{48,40},{56,48},{64,56},{72,6... | collective-permute-start | bytes 73736 | tf_op jit(solution)/shard_map/ppermute | solution.py:10
Sparse Core Ops, SparseCore 0:
  9.8 42.6 all-gather.1
  106.1 39.9 reduce-scatter.1
where the time goes:
time: 275 us; the launch traced here: 271 us
  blocking collectives  128 us (47%)
  local copies, waits for them, and re-layouts  50.9 us (19%)
  matrix products  26.5 us (10%)
  starting transfers between devices  19.7 us (7%)
  waiting for transfers between devices  17.8 us (6%)
  between operations  14.4 us (5%)
  other arithmetic  13.9 us (5%)
    psum x1, blocking collectives, on_device(): filter_grad = lax.psum(diagonals, 'ctx') * norm_factor  128 us
    ppermute x4, starting transfers between devices, from_behind(): return lax.ppermute(block, axis, route)  19.6 us
    reshape x1, local copies, waits for them, and re-layouts, toeplitz(): return tiled.reshape(groups, long_taps, 2 * long_taps - 1)  15.8 us
    all_gather x1, waiting for transfers between devices, on_device(): lax.all_gather(out_cotangent, 'tp', axis=1, tiled=True)  11 us
    reshape x1, local copies, waits for them, and re-layouts, on_device(): correlation.reshape(groups, long_taps * (2 * long_taps - 1))  9.22 us
    dot_general x1, matrix products, on_device(): jnp.dot(mixer, out_weight, preferred_element_type=jnp.float32)  7.74 us
    dot_general x1, matrix products, on_device(): jnp.einsum('tw,cw->tc', lax.all_gather(out_cotangent, 'tp', axis=1, tiled...  7.35 us
    unnamed x22, local copies, waits for them, and re-layouts  7.34 us
  transfers between devices with their start and end apart: 6, of which 2 were waited for; matrix products, arithmetic and copies ran while one was open for 22% of the time, Pallas kernels for 0%

commit v1 on v0

v1 whole, which is shorter than its diff:
```python
import functools

import jax
import jax.numpy as jnp
from jax import lax
from jax.experimental import pallas as pl
from jax.experimental.pallas import tpu as pltpu
from jax.sharding import PartitionSpec as P

MESH = pl.DeviceIdType.MESH
F32 = jnp.float32
BF16 = jnp.bfloat16
ROWS = 256
HALF = 128
CHAN = 1024
OUT = 512
N_TP = 8
N_CTX = 32
GROUPS = 64
QR = 48
PR = HALF - QR
TILES = CHAN // 128
PER = 8
CHIPS = N_CTX // 2


def dot(a, b, dims=((1,), (0,))):
    return lax.dot_general(a, b, (dims, ((), ())), preferred_element_type=F32)


def kernel(
    feat,
    sf,
    lf,
    w_hbm,
    cot,
    mixed,
    fgrads,
    filt,
    feats,
    post,
    gated,
    long_out,
    mixer,
    toep,
    vec_a,
    vec_b,
    gath,
    w,
    psum_p,
    psum_q,
    in_up,
    in_own_dn,
    in_own_up,
    in_x,
    in_q,
    in_q_up,
    in_q_own_dn,
    in_q_own_up,
    d_long,
    d_post,
    corr,
    fpart,
    fcore,
    fsum,
    fall,
    fout,
    out_mixed,
    out_grads,
    lsem,
    ag_s,
    ag_r,
    rs_s,
    rs_r,
    halo_s,
    halo_r,
    fg_s,
    fg_r,
):
    ctx = lax.axis_index("ctx")
    me = lax.axis_index("tp")
    core = lax.rem(ctx, 2)
    chip = ctx // 2
    xl = me // 4
    yl = lax.rem(me, 4)
    step = 1 + 2 * core
    back = 3 - 2 * core
    y_up = lax.rem(yl + step, 4)
    y_dn = lax.rem(yl + back, 4)
    y_op = lax.rem(yl + 2, 4)
    own_base = xl * 4
    x_base = 4 - xl * 4
    up = own_base + y_up
    dn = own_base + y_dn
    op = own_base + y_op
    xo = x_base + yl
    xup = x_base + y_up
    xdn = x_base + y_dn
    xop = x_base + y_op
    nxt = lax.rem(ctx + 1, N_CTX)
    prv = lax.rem(ctx + N_CTX - 1, N_CTX)

    load_f = pltpu.make_async_copy(feat, feats.at[:, pl.ds(16, ROWS), :], lsem.at[0])
    load_w = pltpu.make_async_copy(w_hbm, w, lsem.at[1])
    load_c = pltpu.make_async_copy(cot, gath.at[me], lsem.at[2])
    load_f.start()
    load_w.start()
    load_c.start()

    barrier = pltpu.get_barrier_semaphore()
    peers = [(ctx, xo), (ctx, up), (ctx, dn), (nxt, me), (prv, me)]
    for i in range(1, CHIPS):
        peers.append((2 * lax.rem(chip + i, CHIPS) + core, me))
    for peer in peers:
        pl.semaphore_signal(barrier, inc=1, device_id=peer, device_id_type=MESH)

    rows_i = lax.broadcasted_iota(jnp.int32, (HALF, 2 * HALF), 0)
    cols_i = lax.broadcasted_iota(jnp.int32, (HALF, 2 * HALF), 1)
    flip = (cols_i == HALF - rows_i).astype(BF16)
    keep = (cols_i == rows_i).astype(BF16)
    vec_a[...] = dot(lf[...], flip)
    vec_b[...] = dot(lf[...], keep)
    pl.semaphore_wait(barrier, len(peers))

    started = []

    def remote(src, dst, send, recv, dev):
        return pltpu.make_async_remote_copy(
            src_ref=src,
            dst_ref=dst,
            send_sem=send,
            recv_sem=recv,
            device_id=dev,
            device_id_type=MESH,
        )

    QS = (0, QR)
    PS = (QR, PR)

    def ag_view(slot, half, part):
        return gath.at[slot, pl.ds(half * HALF + part[0], part[1]), :]

    def ag_send(n, half, slot, part, dev, src=None):
        there = ag_view(slot, half, part)
        copy = remote(
            there if src is None else src,
            there,
            ag_s.at[half, n],
            ag_r.at[half, n],
            (ctx, dev),
        )
        copy.start()
        started.append(copy)

    def ag_wait(n, half, slot, part):
        there = ag_view(slot, half, part)
        remote(there, there, ag_s.at[half, n], ag_r.at[half, n], (ctx, xo)).wait_recv()

    def cot_view(half, part):
        return cot.at[pl.ds(half * HALF + part[0], part[1]), :]

    def ag_own(half):
        ag_send(0, half, me, PS, xo, cot_view(half, PS))
        ag_send(2, half, me, QS, up, cot_view(half, QS))
        ag_send(3, half, me, QS, dn, cot_view(half, QS))
        ag_send(1, half, me, QS, xo, cot_view(half, QS))
        ag_send(4, half, me, PS, up, cot_view(half, PS))
        ag_send(5, half, me, PS, dn, cot_view(half, PS))

    def ag_first(half):
        ag_wait(0, half, xo, PS)
        ag_send(6, half, xo, PS, up)
        ag_send(7, half, xo, PS, dn)
        ag_wait(2, half, dn, QS)
        ag_send(8, half, dn, QS, up)
        ag_send(9, half, dn, QS, xo)
        ag_wait(3, half, up, QS)
        ag_send(10, half, up, QS, xo)

    def ag_second(half):
        ag_wait(4, half, dn, PS)
        ag_send(11, half, dn, PS, up)
        ag_wait(8, half, op, QS)
        ag_send(12, half, op, QS, xo)
        ag_wait(6, half, xdn, PS)
        ag_send(13, half, xdn, PS, up)

    def ag_rest(half):
        ag_wait(1, half, xo, QS)
        ag_wait(5, half, up, PS)
        ag_wait(7, half, xup, PS)
        ag_wait(9, half, xdn, QS)
        ag_wait(10, half, xup, QS)
        ag_wait(11, half, op, PS)
        ag_wait(12, half, xop, QS)
        ag_wait(13, half, xop, PS)

    ag_own(0)
    feat_halo = remote(
        feat.at[:, pl.ds(ROWS - 16, 16), :],
        feats.at[:, pl.ds(0, 16), :],
        halo_s.at[0],
        halo_r.at[0],
        (nxt, me),
    )
    feat_halo.start()
    started.append(feat_halo)
    ag_own(1)

    def short_conv(half):
        r0 = half * HALF

        def tile(c, carry):
            lanes = pl.ds(pl.multiple_of(c * 128, 128), 128)
            kept = []
            for i in range(3):
                ext = feats[i, pl.ds(r0, HALF + 16), lanes].astype(F32)
                taps = sf[i, :, lanes].astype(F32)
                value = (
                    taps[0:1] * ext[16 : 16 + HALF]
                    + taps[1:2] * ext[15 : 15 + HALF]
                    + taps[2:3] * ext[14 : 14 + HALF]
                ).astype(BF16)
                post[i, pl.ds(r0, HALF), lanes] = value
                kept.append(value.astype(F32))
            gated[pl.ds(HALF + r0, HALF), lanes] = (kept[1] * kept[2]).astype(BF16)
            return carry

        lax.fori_loop(0, TILES, tile, 0)

    load_f.wait()
    short_conv(1)
    gated_halo = remote(
        gated.at[pl.ds(2 * HALF, HALF), :],
        gated.at[pl.ds(0, HALF), :],
        halo_s.at[1],
        halo_r.at[1],
        (nxt, me),
    )
    gated_halo.start()
    started.append(gated_halo)
    feat_halo.wait_recv()

    @pl.when(ctx == 0)
    def _():
        feats[:, 0:16, :] = jnp.zeros((3, 16, CHAN), BF16)

    short_conv(0)

    def build(vec):
        def group(g, carry):
            row = jnp.broadcast_to(vec[pl.ds(g, 1), :], (HALF, 2 * HALF))
            there = pl.ds(pl.multiple_of(g * HALF, HALF), HALF)
            toep[there, :] = pltpu.roll(row, 0, 1, stride=1, stride_axis=0).astype(BF16)
            return carry

        lax.fori_loop(0, GROUPS, group, 0)

    lane_group = lax.broadcasted_iota(jnp.int32, (HALF, 128), 1) // 16

    def long_conv(window, c):
        block = toep[pl.ds(pl.multiple_of(c * PER * HALF, PER * HALF), PER * HALF), :]
        whole = dot(block, window)
        out = whole[0:HALF]
        for q in range(1, PER):
            out = jnp.where(lane_group == q, whole[q * HALF : (q + 1) * HALF], out)
        return out

    def forward_conv(half):
        r0 = half * HALF

        def tile(c, carry):
            lanes = pl.ds(pl.multiple_of(c * 128, 128), 128)
            out = long_conv(gated[pl.ds(r0, 2 * HALF), lanes], c)
            long_out[pl.ds(r0, HALF), lanes] = out
            mixer[pl.ds(r0, HALF), lanes] = (
                post[0, pl.ds(r0, HALF), lanes].astype(F32) * out
            ).astype(BF16)
            return carry

        lax.fori_loop(0, TILES, tile, 0)

    build(vec_a)
    ag_first(0)
    forward_conv(1)
    ag_second(0)
    ag_first(1)

    def project(half, side, place, owner):
        cols = pl.ds(pl.multiple_of(owner * OUT, OUT), OUT)
        part = dot(mixer[pl.ds(half * HALF, HALF), :], w[:, cols]).astype(BF16)
        psum_q[half, side, place] = part[0:QR]
        psum_p[half, place, side] = part[QR:HALF]

    def rs_copy(n, half, src, dst, dev):
        return remote(src, dst, rs_s.at[half, n], rs_r.at[half, n], (ctx, dev))

    def rs_all(half):
        copies = [
            rs_copy(0, half, psum_p.at[half, 3], in_up.at[half], up),
            rs_copy(1, half, psum_p.at[half, 2], in_own_up.at[half], dn),
            rs_copy(2, half, psum_q.at[half, 1, 3], in_q.at[half, 3], xo),
            rs_copy(3, half, psum_q.at[half, 1, 2], in_q.at[half, 2], xo),
            rs_copy(4, half, psum_q.at[half, 1, 1], in_q.at[half, 1], xo),
            rs_copy(5, half, psum_q.at[half, 1, 0], in_q.at[half, 0], xo),
            rs_copy(6, half, psum_p.at[half, 1], in_own_dn.at[half], up),
            rs_copy(7, half, psum_q.at[half, 0, 3], in_q_up.at[half], up),
            rs_copy(8, half, psum_q.at[half, 0, 2], in_q_own_up.at[half], dn),
            rs_copy(9, half, psum_q.at[half, 0, 1], in_q_own_dn.at[half], up),
            rs_copy(10, half, psum_p.at[half, 0, 1], in_x.at[half], xo),
        ]
        return copies

    rs = [rs_all(0), rs_all(1)]

    def rs_start(half, n):
        rs[half][n].start()
        started.append(rs[half][n])

    def rs_begin(half):
        project(half, 1, 3, xop)
        rs_start(half, 2)
        project(half, 0, 3, op)
        rs_start(half, 0)
        project(half, 1, 2, xdn)
        rs_start(half, 3)
        project(half, 0, 2, dn)
        rs_start(half, 1)
        project(half, 1, 1, xup)
        rs_start(half, 4)
        project(half, 1, 0, xo)
        rs_start(half, 5)
        project(half, 0, 1, up)
        project(half, 0, 0, me)

    def add(a, *others):
        total = a.astype(F32)
        for other in others:
            total = total + other.astype(F32)
        return total.astype(BF16)

    def rs_first(half):
        rs[half][2].wait_recv()
        psum_q[half, 0, 3] = add(psum_q[half, 0, 3], in_q[half, 3])
        rs_start(half, 7)
        rs[half][0].wait_recv()
        psum_p[half, 1] = add(psum_p[half, 1], in_up[half])
        rs_start(half, 6)
        rs[half][3].wait_recv()
        psum_q[half, 0, 2] = add(psum_q[half, 0, 2], in_q[half, 2])
        rs_start(half, 8)

    def rs_second(half):
        rs[half][4].wait_recv()
        rs[half][7].wait_recv()
        psum_q[half, 0, 1] = add(psum_q[half, 0, 1], in_q[half, 1], in_q_up[half])
        rs_start(half, 9)
        rs[half][1].wait_recv()
        rs[half][6].wait_recv()
        psum_p[half, 0, 1] = add(psum_p[half, 0, 1], in_own_dn[half, 1], in_own_up[half, 1])
        rs_start(half, 10)

    def rs_last(half):
        rs[half][5].wait_recv()
        rs[half][8].wait_recv()
        rs[half][9].wait_recv()
        out_mixed[pl.ds(half * HALF, QR), :] = add(
            psum_q[half, 0, 0], in_q[half, 0], in_q_own_dn[half], in_q_own_up[half]
        )
        rs[half][10].wait_recv()
        out_mixed[pl.ds(half * HALF + QR, PR), :] = add(
            psum_p[half, 0, 0], in_own_dn[half, 0], in_own_up[half, 0], in_x[half]
        )

    load_w.wait()
    rs_begin(1)
    gated_halo.wait_recv()

    @pl.when(ctx == 0)
    def _():
        gated[0:HALF, :] = jnp.zeros((HALF, CHAN), BF16)

    forward_conv(0)
    ag_second(1)
    rs_first(1)
    rs_begin(0)
    build(vec_b)

    def d_mixer(half):
        r0 = half * HALF

        def tile(c, carry):
            chans = pl.ds(pl.multiple_of(c * 256, 256), 256)
            total = jnp.zeros((HALF, 256), F32)
            for s in range(N_TP):
                total = total + dot(
                    gath[s, pl.ds(r0, HALF), :],
                    w[chans, pl.ds(s * OUT, OUT)],
                    ((1,), (1,)),
                )
            grad = total.astype(BF16).astype(F32)
            d_post[0, pl.ds(r0, HALF), chans] = grad * long_out[pl.ds(r0, HALF), chans]
            d_long[pl.ds(r0, HALF), chans] = (
                grad * post[0, pl.ds(r0, HALF), chans].astype(F32)
            ).astype(BF16)
            return carry

        lax.fori_loop(0, CHAN // 256, tile, 0)

    load_c.wait()
    ag_rest(0)
    d_mixer(0)
    long_halo = remote(
        d_long.at[pl.ds(0, HALF), :],
        d_long.at[pl.ds(2 * HALF, HALF), :],
        halo_s.at[2],
        halo_r.at[2],
        (prv, me),
    )
    long_halo.start()
    started.append(long_halo)
    rs_second(1)
    rs_first(0)
    ag_rest(1)
    d_mixer(1)

    back_rows = lax.broadcasted_iota(jnp.int32, (HALF, HALF), 0)
    back_cols = lax.broadcasted_iota(jnp.int32, (HALF, HALF), 1)
    reverse = (back_cols == HALF - 1 - back_rows).astype(BF16)
    wide_group = lax.rem(lax.broadcasted_iota(jnp.int32, (HALF, 256), 1), 128) // 16

    def corr_tile(c, carry):
        lanes = pl.ds(pl.multiple_of(c * 128, 128), 128)
        grads = jnp.concatenate(
            [d_long[pl.ds(0, HALF), lanes], d_long[pl.ds(HALF, HALF), lanes]], axis=1
        )
        grads = dot(reverse, grads)
        window = jnp.concatenate(
            [gated[pl.ds(0, 2 * HALF), lanes], gated[pl.ds(HALF, 2 * HALF), lanes]], axis=1
        )
        stack = jnp.concatenate(
            [jnp.where(wide_group == q, grads, 0.0).astype(BF16) for q in range(PER)], axis=0
        )
        whole = dot(stack, window, ((1,), (1,)))
        sums = []
        for q in range(PER):
            rolled = pltpu.roll(
                whole[q * HALF : (q + 1) * HALF], HALF + 1, 1, stride=1, stride_axis=0
            )
            sums.append(jnp.sum(rolled, axis=0, keepdims=True))
        corr[pl.ds(pl.multiple_of(c * PER, PER), PER), :] = jnp.concatenate(sums, axis=0)
        return carry

    lax.fori_loop(0, TILES, corr_tile, 0)
    fpart[...] = lax.dot_general(
        corr[...],
        (cols_i == HALF - rows_i).astype(F32),
        (((1,), (1,)), ((), ())),
        preferred_element_type=F32,
        precision=lax.Precision.HIGHEST,
    ).reshape(2, GROUPS // 2, HALF)
    sibling = (ctx + 1 - 2 * core, me)
    f_core = remote(fpart.at[1 - core], fcore, fg_s.at[0], fg_r.at[0], sibling)
    f_core.start()
    started.append(f_core)

    def backward_conv(half):
        r0 = half * HALF

        def tile(c, carry):
            lanes = pl.ds(pl.multiple_of(c * 128, 128), 128)
            out = long_conv(d_long[pl.ds(r0, 2 * HALF), lanes], c)
            for i in (1, 2):
                d_post[i, pl.ds(r0, HALF), lanes] = out * post[
                    3 - i, pl.ds(r0, HALF), lanes
                ].astype(F32)
            return carry

        lax.fori_loop(0, TILES, tile, 0)

    backward_conv(0)
    post_halo = remote(
        d_post.at[:, pl.ds(0, 8), :],
        d_post.at[:, pl.ds(ROWS, 8), :],
        halo_s.at[3],
        halo_r.at[3],
        (prv, me),
    )
    post_halo.start()
    started.append(post_halo)

    f_core.wait_recv()
    fsum[...] = fpart[core] + fcore[...]
    f_all = []
    for i in range(1, CHIPS):
        copy = remote(
            fsum,
            fall.at[chip],
            fg_s.at[i],
            fg_r.at[i],
            (2 * lax.rem(chip + i, CHIPS) + core, me),
        )
        copy.start()
        started.append(copy)

    rs_second(0)
    long_halo.wait_recv()

    @pl.when(ctx == N_CTX - 1)
    def _():
        d_long[2 * HALF : 3 * HALF, :] = jnp.zeros((HALF, CHAN), BF16)

    backward_conv(1)
    post_halo.wait_recv()

    @pl.when(ctx == N_CTX - 1)
    def _():
        d_post[:, ROWS : ROWS + 8, :] = jnp.zeros((3, 8, CHAN), F32)

    def short_back(half):
        r0 = half * HALF

        def tile(c, carry):
            lanes = pl.ds(pl.multiple_of(c * 128, 128), 128)
            for i in range(3):
                ext = d_post[i, pl.ds(r0, HALF + 8), lanes]
                taps = sf[i, :, lanes].astype(F32)
                out_grads[i, pl.ds(r0, HALF), lanes] = (
                    taps[0:1] * ext[0:HALF]
                    + taps[1:2] * ext[1 : 1 + HALF]
                    + taps[2:3] * ext[2 : 2 + HALF]
                ).astype(BF16)
            return carry

        lax.fori_loop(0, TILES, tile, 0)

    short_back(0)
    short_back(1)
    store_g = pltpu.make_async_copy(out_grads, fgrads, lsem.at[3])
    store_g.start()

    total = fsum[...]
    for i in range(1, CHIPS):
        slot = lax.rem(chip + CHIPS - i, CHIPS)
        remote(fsum, fall.at[slot], fg_s.at[i], fg_r.at[i], sibling).wait_recv()
        total = total + fall[slot]
    fout[core] = total * ((N_CTX * ROWS * 16) ** -0.5)
    f_out = remote(fout.at[core], fout.at[core], fg_s.at[16], fg_r.at[16], sibling)
    f_out.start()
    started.append(f_out)

    rs_last(1)
    rs_last(0)
    store_m = pltpu.make_async_copy(out_mixed, mixed, lsem.at[4])
    store_m.start()
    remote(
        fout.at[1 - core], fout.at[1 - core], fg_s.at[16], fg_r.at[16], sibling
    ).wait_recv()
    filt[...] = fout[...].reshape(GROUPS, HALF)

    for copy in started:
        copy.wait_send()
    store_g.wait()
    store_m.wait()


def on_device(features, short_filter, long_filter, out_weight, out_cotangent):
    hbm = pl.BlockSpec(memory_space=pl.ANY)
    vmem = pl.BlockSpec(memory_space=pltpu.VMEM)
    dma = pltpu.SemaphoreType.DMA
    scratch = [
        pltpu.VMEM((3, ROWS + 16, CHAN), BF16),
        pltpu.VMEM((3, ROWS, CHAN), BF16),
        pltpu.VMEM((ROWS + HALF, CHAN), BF16),
        pltpu.VMEM((ROWS, CHAN), F32),
        pltpu.VMEM((ROWS, CHAN), BF16),
        pltpu.VMEM((GROUPS * HALF, 2 * HALF), BF16),
        pltpu.VMEM((GROUPS, 2 * HALF), F32),
        pltpu.VMEM((GROUPS, 2 * HALF), F32),
        pltpu.VMEM((N_TP, ROWS, OUT), BF16),
        pltpu.VMEM((CHAN, N_TP * OUT), BF16),
        pltpu.VMEM((2, 4, 2, PR, OUT), BF16),
        pltpu.VMEM((2, 2, 4, QR, OUT), BF16),
        pltpu.VMEM((2, 2, PR, OUT), BF16),
        pltpu.VMEM((2, 2, PR, OUT), BF16),
        pltpu.VMEM((2, 2, PR, OUT), BF16),
        pltpu.VMEM((2, PR, OUT), BF16),
        pltpu.VMEM((2, 4, QR, OUT), BF16),
        pltpu.VMEM((2, QR, OUT), BF16),
        pltpu.VMEM((2, QR, OUT), BF16),
        pltpu.VMEM((2, QR, OUT), BF16),
        pltpu.VMEM((ROWS + HALF, CHAN), BF16),
        pltpu.VMEM((3, ROWS + 8, CHAN), F32),
        pltpu.VMEM((GROUPS, 2 * HALF), F32),
        pltpu.VMEM((2, GROUPS // 2, HALF), F32),
        pltpu.VMEM((GROUPS // 2, HALF), F32),
        pltpu.VMEM((GROUPS // 2, HALF), F32),
        pltpu.VMEM((CHIPS, GROUPS // 2, HALF), F32),
        pltpu.VMEM((2, GROUPS // 2, HALF), F32),
        pltpu.VMEM((ROWS, OUT), BF16),
        pltpu.VMEM((3, ROWS, CHAN), BF16),
        dma((5,)),
        dma((2, 14)),
        dma((2, 14)),
        dma((2, 11)),
        dma((2, 11)),
        dma((4,)),
        dma((4,)),
        dma((17,)),
        dma((17,)),
    ]
    return pl.pallas_call(
        kernel,
        out_shape=(
            jax.ShapeDtypeStruct((ROWS, OUT), BF16),
            jax.ShapeDtypeStruct((3, ROWS, CHAN), BF16),
            jax.ShapeDtypeStruct((GROUPS, HALF), F32),
        ),
        in_specs=[hbm, vmem, vmem, hbm, hbm],
        out_specs=(hbm, hbm, vmem),
        scratch_shapes=scratch,
        compiler_params=pltpu.CompilerParams(
            collective_id=0, has_side_effects=True, vmem_limit_bytes=56 * 2**20
        ),
    )(features, short_filter, long_filter, out_weight, out_cotangent)


def solution(mesh):
    placed = (
        P(None, "ctx", "tp"),
        P(None, None, "tp"),
        P("tp", None),
        P("tp", None),
        P("ctx", "tp"),
    )
    return jax.shard_map(
        on_device,
        mesh=mesh,
        in_specs=placed,
        out_specs=(P("ctx", "tp"), P(None, "ctx", "tp"), P("tp", None)),
        check_vma=False,
    )
```

time: 275 us -> 77.6 us (0.28); the launches traced: 271 us -> 77.4 us
  blocking collectives: 128 us -> 0 us
  Pallas kernels: 0 us -> 71.8 us
  local copies, waits for them, and re-layouts: 50.9 us -> 4.96 us
  matrix products: 26.5 us -> 0 us
  starting transfers between devices: 19.7 us -> 0 us
  waiting for transfers between devices: 17.8 us -> 0 us
  other arithmetic: 13.9 us -> 0 us
  between operations: 14.4 us -> 0.64 us
    psum x1 -> x0, blocking collectives: 128 us -> none  [on_device(): filter_grad = lax.psum(diagonals, 'ctx') * norm_factor]
    pallas_call x0 -> x1, Pallas kernels: none -> 71.8 us  [on_device(): pl.pallas_call(kernel, out_shape=(jax.ShapeDtypeStruct((ROWS, OUT), BF16)...]
    reshape x4 -> x0, local copies, waits for them, and re-layouts: 26.7 us -> none  [the longest x1 15.8 us: toeplitz(): return tiled.reshape(groups, long_taps, 2 * long_taps - 1)]
    dot_general x5 -> x0, matrix products: 26.5 us -> none  [the longest x1 7.74 us: on_device(): jnp.dot(mixer, out_weight, preferred_element_type=jnp.float32)]
    ppermute x4 -> x0, starting transfers between devices: 19.6 us -> none  [from_behind(): return lax.ppermute(block, axis, route)]
    all_gather x1 -> x0, waiting for transfers between devices: 11 us -> none  [on_device(): lax.all_gather(out_cotangent, 'tp', axis=1, tiled=True)]
    convert_element_type x2 -> x0, other arithmetic: 6.12 us -> none  [the longest x1 3.97 us: on_device(): post_float = post.astype(jnp.float32)]
    ppermute x4 -> x0, waiting for transfers between devices: 6.11 us -> none  [from_behind(): return lax.ppermute(block, axis, route)]
  transfers between devices with their start and end apart: 6 -> 0, of which waited for: 2 -> 0; matrix products, arithmetic and copies ran while one was open for 22% -> 0% of each run, Pallas kernels for 0% -> 0%
where the time goes in v1:
time: 77.6 us; the launch traced here: 77.4 us
  Pallas kernels  71.8 us (93%)
  local copies, waits for them, and re-layouts  4.96 us (6%)
    pallas_call x1, Pallas kernels, on_device(): pl.pallas_call(kernel, out_shape=(jax.ShapeDtypeStruct((ROWS, OUT), BF16)...  71.8 us
    unnamed x5, local copies, waits for them, and re-layouts  4.96 us

profile of v1, /device:TPU:1, one launch (start us, length us, event | category | flops | bytes accessed | tf_op | source)
XLA Modules:
  0.0 77.4 jit_solution(12270003452441766594)
XLA Ops:
  0.6 71.8 %shard_map.76 = (bf16[256,512]{1,0:T(8,128)(2,1)}, bf16[3,256,1024]{2,1,0:T(8,128)(2,1)}, f32[64,128]{1,0:T(8,128)}) custom-call(bf16[3,256,1024]{2,1,0:T(8,128)(2,1)} %feat.1, bf16[3,3,1024]{2,1,0:T(4,128)(2,1)} %sf.1, bf16[64,128]{1,0:T(8,128)(2,1)} %lf.1, bf16[1024,4096]{1,0:T(8,128)(2,1)} %w_hbm.1, bf16[256,512]{1,0:T(8,128)(2,1)} %cot.1), custom_call_target="tpu_custom_call" | custom-call | tf_op jit(solution)/shard_map/pallas_call | solution.py:612
  72.5 1.7 %copy.11 = bf16[256,512]{1,0:T(8,128)(2,1)} copy(bf16[256,512]{1,0:T(8,128)(2,1)} %get-tuple-element.6) | data formatting | bytes 524288
  74.1 0.0 copy-start
  74.1 2.7 %copy.12 = bf16[3,256,1024]{2,1,0:T(8,128)(2,1)} copy(bf16[3,256,1024]{2,1,0:T(8,128)(2,1)} %get-tuple-element.7) | data formatting | bytes 3145728
  76.8 0.0 copy-done
  76.8 0.6 copy.13
Async XLA Ops:
  74.1 2.7 %copy-start = (f32[64,128]{1,0:T(8,128)S(1)}, f32[64,128]{1,0:T(8,128)}, u32[]{:S(2)}) copy-start(f32[64,128]{1,0:T(8,128)} %get-tuple-element.8) | copy-start | bytes 98308

commit v2 on v1

--- a/solution.py
+++ b/solution.py
@@ -21,7 +21,12 @@
 PR = HALF - QR
 TILES = CHAN // 128
 PER = 8
-CHIPS = N_CTX // 2
+QUAD = 4
+RINGS = N_CTX // QUAD
+SHARE = GROUPS // QUAD
+STEP = 16
+SPAN = HALF + STEP
+STEPS = HALF // STEP
 
 
 def dot(a, b, dims=((1,), (0,))):
@@ -42,7 +47,8 @@
     gated,
     long_out,
     mixer,
-    toep,
+    toep_a,
+    toep_b,
     vec_a,
     vec_b,
     gath,
@@ -59,7 +65,9 @@
     in_q_own_up,
     d_long,
     d_post,
-    corr,
+    corr_lo,
+    corr_hi,
+    d_acc,
     fpart,
     fcore,
     fsum,
@@ -80,7 +88,9 @@
     ctx = lax.axis_index("ctx")
     me = lax.axis_index("tp")
     core = lax.rem(ctx, 2)
-    chip = ctx // 2
+    quad = lax.rem(ctx, QUAD)
+    ring = ctx // QUAD
+    corner = ctx - quad
     xl = me // 4
     yl = lax.rem(me, 4)
     step = 1 + 2 * core
@@ -108,9 +118,11 @@
     load_c.start()
 
     barrier = pltpu.get_barrier_semaphore()
-    peers = [(ctx, xo), (ctx, up), (ctx, dn), (nxt, me), (prv, me)]
-    for i in range(1, CHIPS):
-        peers.append((2 * lax.rem(chip + i, CHIPS) + core, me))
+    across = core * nxt + (1 - core) * prv
+    quads = [corner + lax.rem(quad + k, QUAD) for k in range(1, QUAD)]
+    along = [lax.rem(ring + k, RINGS) * QUAD + quad for k in range(1, RINGS)]
+    peers = [(ctx, xo), (ctx, up), (ctx, dn), (across, me)]
+    peers += [(dev, me) for dev in quads + along]
     for peer in peers:
         pl.semaphore_signal(barrier, inc=1, device_id=peer, device_id_type=MESH)
 
@@ -120,6 +132,17 @@
     keep = (cols_i == rows_i).astype(BF16)
     vec_a[...] = dot(lf[...], flip)
     vec_b[...] = dot(lf[...], keep)
+
+    def build(vec, toep):
+        def group(g, carry):
+            row = jnp.broadcast_to(vec[pl.ds(g, 1), :], (STEP, 2 * HALF))
+            there = pl.ds(pl.multiple_of(g * STEP, STEP), STEP)
+            toep[there, :] = pltpu.roll(row, 0, 1, stride=1, stride_axis=0).astype(BF16)
+            return carry
+
+        lax.fori_loop(0, GROUPS, group, 0, unroll=8)
+
+    build(vec_a, toep_a)
     pl.semaphore_wait(barrier, len(peers))
 
     started = []
@@ -168,26 +191,30 @@
         ag_send(5, half, me, PS, dn, cot_view(half, PS))
 
     def ag_first(half):
-        ag_wait(0, half, xo, PS)
-        ag_send(6, half, xo, PS, up)
-        ag_send(7, half, xo, PS, dn)
         ag_wait(2, half, dn, QS)
         ag_send(8, half, dn, QS, up)
         ag_send(9, half, dn, QS, xo)
         ag_wait(3, half, up, QS)
         ag_send(10, half, up, QS, xo)
+        ag_wait(0, half, xo, PS)
+        ag_send(6, half, xo, PS, up)
+        ag_send(7, half, xo, PS, dn)
 
     def ag_second(half):
         ag_wait(4, half, dn, PS)
         ag_send(11, half, dn, PS, up)
+
+    def ag_third(half):
         ag_wait(8, half, op, QS)
         ag_send(12, half, op, QS, xo)
         ag_wait(6, half, xdn, PS)
         ag_send(13, half, xdn, PS, up)
 
-    def ag_rest(half):
+    def ag_near(half):
         ag_wait(1, half, xo, QS)
         ag_wait(5, half, up, PS)
+
+    def ag_rest(half):
         ag_wait(7, half, xup, PS)
         ag_wait(9, half, xdn, QS)
         ag_wait(10, half, xup, QS)
@@ -195,7 +222,6 @@
         ag_wait(12, half, xop, QS)
         ag_wait(13, half, xop, PS)
 
-    ag_own(0)
     feat_halo = remote(
         feat.at[:, pl.ds(ROWS - 16, 16), :],
         feats.at[:, pl.ds(0, 16), :],
@@ -205,7 +231,7 @@
     )
     feat_halo.start()
     started.append(feat_halo)
-    ag_own(1)
+    ag_own(0)
 
     def short_conv(half):
         r0 = half * HALF
@@ -226,7 +252,7 @@
             gated[pl.ds(HALF + r0, HALF), lanes] = (kept[1] * kept[2]).astype(BF16)
             return carry
 
-        lax.fori_loop(0, TILES, tile, 0)
+        lax.fori_loop(0, TILES, tile, 0, unroll=True)
 
     load_f.wait()
     short_conv(1)
@@ -239,6 +265,9 @@
     )
     gated_halo.start()
     started.append(gated_halo)
+    ag_own(1)
+    build(vec_b, toep_b)
+    ag_first(0)
     feat_halo.wait_recv()
 
     @pl.when(ctx == 0)
@@ -246,45 +275,40 @@
         feats[:, 0:16, :] = jnp.zeros((3, 16, CHAN), BF16)
 
     short_conv(0)
-
-    def build(vec):
-        def group(g, carry):
-            row = jnp.broadcast_to(vec[pl.ds(g, 1), :], (HALF, 2 * HALF))
-            there = pl.ds(pl.multiple_of(g * HALF, HALF), HALF)
-            toep[there, :] = pltpu.roll(row, 0, 1, stride=1, stride_axis=0).astype(BF16)
-            return carry
-
-        lax.fori_loop(0, GROUPS, group, 0)
-
-    lane_group = lax.broadcasted_iota(jnp.int32, (HALF, 128), 1) // 16
-
-    def long_conv(window, c):
-        block = toep[pl.ds(pl.multiple_of(c * PER * HALF, PER * HALF), PER * HALF), :]
+    ag_second(0)
+
+    lane_group = lax.broadcasted_iota(jnp.int32, (STEP, 128), 1) // 16
+
+    def long_conv(toep, source, r0, c, lanes):
+        block = toep[pl.ds(pl.multiple_of(c * HALF, HALF), HALF), 0:SPAN]
+        window = jnp.concatenate(
+            [source[pl.ds(r0 + STEP * a, SPAN), lanes] for a in range(STEPS)], axis=1
+        )
         whole = dot(block, window)
-        out = whole[0:HALF]
-        for q in range(1, PER):
-            out = jnp.where(lane_group == q, whole[q * HALF : (q + 1) * HALF], out)
-        return out
+        outs = []
+        for a in range(STEPS):
+            cols = slice(a * 128, (a + 1) * 128)
+            out = whole[0:STEP, cols]
+            for q in range(1, PER):
+                out = jnp.where(lane_group == q, whole[q * STEP : (q + 1) * STEP, cols], out)
+            outs.append(out)
+        return jnp.concatenate(outs, axis=0)
 
     def forward_conv(half):
         r0 = half * HALF
 
         def tile(c, carry):
             lanes = pl.ds(pl.multiple_of(c * 128, 128), 128)
-            out = long_conv(gated[pl.ds(r0, 2 * HALF), lanes], c)
+            out = long_conv(toep_a, gated, r0, c, lanes)
             long_out[pl.ds(r0, HALF), lanes] = out
             mixer[pl.ds(r0, HALF), lanes] = (
                 post[0, pl.ds(r0, HALF), lanes].astype(F32) * out
             ).astype(BF16)
             return carry
 
-        lax.fori_loop(0, TILES, tile, 0)
-
-    build(vec_a)
-    ag_first(0)
+        lax.fori_loop(0, TILES, tile, 0, unroll=True)
+
     forward_conv(1)
-    ag_second(0)
-    ag_first(1)
 
     def project(half, side, place, owner):
         cols = pl.ds(pl.multiple_of(owner * OUT, OUT), OUT)
@@ -317,21 +341,19 @@
         rs[half][n].start()
         started.append(rs[half][n])
 
-    def rs_begin(half):
+    def project_all(half):
         project(half, 1, 3, xop)
-        rs_start(half, 2)
         project(half, 0, 3, op)
-        rs_start(half, 0)
         project(half, 1, 2, xdn)
-        rs_start(half, 3)
         project(half, 0, 2, dn)
-        rs_start(half, 1)
         project(half, 1, 1, xup)
-        rs_start(half, 4)
         project(half, 1, 0, xo)
-        rs_start(half, 5)
         project(half, 0, 1, up)
         project(half, 0, 0, me)
+
+    def rs_begin(half):
+        for n in (2, 0, 3, 1, 4, 5):
+            rs_start(half, n)
 
     def add(a, *others):
         total = a.astype(F32)
@@ -373,7 +395,9 @@
         )
 
     load_w.wait()
-    rs_begin(1)
+    project_all(1)
+    ag_third(0)
+    ag_first(1)
     gated_halo.wait_recv()
 
     @pl.when(ctx == 0)
@@ -382,34 +406,33 @@
 
     forward_conv(0)
     ag_second(1)
-    rs_first(1)
+    project_all(0)
+    rs_begin(1)
+    ag_third(1)
     rs_begin(0)
-    build(vec_b)
-
-    def d_mixer(half):
+
+    def d_mixer(half, slots, first, last):
         r0 = half * HALF
-
-        def tile(c, carry):
-            chans = pl.ds(pl.multiple_of(c * 256, 256), 256)
-            total = jnp.zeros((HALF, 256), F32)
-            for s in range(N_TP):
-                total = total + dot(
-                    gath[s, pl.ds(r0, HALF), :],
-                    w[chans, pl.ds(s * OUT, OUT)],
-                    ((1,), (1,)),
-                )
-            grad = total.astype(BF16).astype(F32)
+        for c in range(CHAN // 256):
+            chans = pl.ds(c * 256, 256)
+            total = None if first else d_acc[chans, :]
+            for s in slots:
+                cols = pl.ds(pl.multiple_of(s * OUT, OUT), OUT)
+                part = dot(w[chans, cols], gath[s, pl.ds(r0, HALF), :], ((1,), (1,)))
+                total = part if total is None else total + part
+            if not last:
+                d_acc[chans, :] = total
+                continue
+            grad = total.T.astype(BF16).astype(F32)
             d_post[0, pl.ds(r0, HALF), chans] = grad * long_out[pl.ds(r0, HALF), chans]
             d_long[pl.ds(r0, HALF), chans] = (
                 grad * post[0, pl.ds(r0, HALF), chans].astype(F32)
             ).astype(BF16)
-            return carry
-
-        lax.fori_loop(0, CHAN // 256, tile, 0)
 
     load_c.wait()
+    ag_near(0)
     ag_rest(0)
-    d_mixer(0)
+    d_mixer(0, range(N_TP), True, True)
     long_halo = remote(
         d_long.at[pl.ds(0, HALF), :],
         d_long.at[pl.ds(2 * HALF, HALF), :],
@@ -419,64 +442,78 @@
     )
     long_halo.start()
     started.append(long_halo)
-    rs_second(1)
+    rs_first(1)
+
+    wide_group = lax.rem(lax.broadcasted_iota(jnp.int32, (STEP, CHAN), 1), 128) // 16
+
+    def correlate(half):
+        r0 = half * HALF
+        for c in range(TILES):
+            lanes = pl.ds(c * 128, 128)
+            grads = jnp.concatenate(
+                [d_long[pl.ds(r0 + STEP * a, STEP), lanes] for a in range(STEPS)], axis=1
+            )
+            stack = jnp.concatenate(
+                [jnp.where(wide_group == q, grads, jnp.zeros_like(grads)) for q in range(PER)],
+                axis=0,
+            )
+            window = jnp.concatenate(
+                [gated[pl.ds(r0 + STEP * a, SPAN), lanes] for a in range(STEPS)], axis=1
+            )
+            whole = dot(stack, window, ((1,), (1,)))
+            there = pl.ds(c * HALF, HALF)
+            if half == 0:
+                corr_lo[there, :] = whole[:, 0:128]
+                corr_hi[there, 0:STEP] = whole[:, 128:SPAN]
+            else:
+                corr_lo[there, :] = corr_lo[there, :] + whole[:, 0:128]
+                corr_hi[there, 0:STEP] = corr_hi[there, 0:STEP] + whole[:, 128:SPAN]
+
+    def corr_row(b):
+        rows = pl.ds(b, GROUPS, stride=STEP)
+        return jnp.concatenate([corr_lo[rows, :], corr_hi[rows, :]], axis=1)
+
+    ag_near(1)
+    d_mixer(1, (me, xo, up, dn), True, False)
     rs_first(0)
+    correlate(0)
     ag_rest(1)
-    d_mixer(1)
-
-    back_rows = lax.broadcasted_iota(jnp.int32, (HALF, HALF), 0)
-    back_cols = lax.broadcasted_iota(jnp.int32, (HALF, HALF), 1)
-    reverse = (back_cols == HALF - 1 - back_rows).astype(BF16)
-    wide_group = lax.rem(lax.broadcasted_iota(jnp.int32, (HALF, 256), 1), 128) // 16
-
-    def corr_tile(c, carry):
-        lanes = pl.ds(pl.multiple_of(c * 128, 128), 128)
-        grads = jnp.concatenate(
-            [d_long[pl.ds(0, HALF), lanes], d_long[pl.ds(HALF, HALF), lanes]], axis=1
-        )
-        grads = dot(reverse, grads)
-        window = jnp.concatenate(
-            [gated[pl.ds(0, 2 * HALF), lanes], gated[pl.ds(HALF, 2 * HALF), lanes]], axis=1
-        )
-        stack = jnp.concatenate(
-            [jnp.where(wide_group == q, grads, 0.0).astype(BF16) for q in range(PER)], axis=0
-        )
-        whole = dot(stack, window, ((1,), (1,)))
-        sums = []
-        for q in range(PER):
-            rolled = pltpu.roll(
-                whole[q * HALF : (q + 1) * HALF], HALF + 1, 1, stride=1, stride_axis=0
-            )
-            sums.append(jnp.sum(rolled, axis=0, keepdims=True))
-        corr[pl.ds(pl.multiple_of(c * PER, PER), PER), :] = jnp.concatenate(sums, axis=0)
-        return carry
-
-    lax.fori_loop(0, TILES, corr_tile, 0)
+    d_mixer(1, (xup, xdn, op, xop), False, True)
+    correlate(1)
+    taps_sum = corr_row(0)
+    for b in range(1, STEP):
+        taps_sum = taps_sum + pltpu.roll(corr_row(b), 2 * HALF - b, 1)
+    lane_i = lax.broadcasted_iota(jnp.int32, (GROUPS, 2 * HALF), 1)
+    taps_sum = jnp.where((lane_i >= 1) & (lane_i <= HALF), taps_sum, 0.0)
     fpart[...] = lax.dot_general(
-        corr[...],
+        taps_sum,
         (cols_i == HALF - rows_i).astype(F32),
         (((1,), (1,)), ((), ())),
         preferred_element_type=F32,
         precision=lax.Precision.HIGHEST,
-    ).reshape(2, GROUPS // 2, HALF)
-    sibling = (ctx + 1 - 2 * core, me)
-    f_core = remote(fpart.at[1 - core], fcore, fg_s.at[0], fg_r.at[0], sibling)
-    f_core.start()
-    started.append(f_core)
+    ).reshape(QUAD, SHARE, HALF)
+    for k in range(1, QUAD):
+        there = lax.rem(quad + k, QUAD)
+        copy = remote(
+            fpart.at[there], fcore.at[quad], fg_s.at[k], fg_r.at[k], (quads[k - 1], me)
+        )
+        copy.start()
+        started.append(copy)
+    rs_second(1)
 
     def backward_conv(half):
         r0 = half * HALF
 
         def tile(c, carry):
             lanes = pl.ds(pl.multiple_of(c * 128, 128), 128)
-            out = long_conv(d_long[pl.ds(r0, 2 * HALF), lanes], c)
+            out = long_conv(toep_b, d_long, r0, c, lanes)
             for i in (1, 2):
                 d_post[i, pl.ds(r0, HALF), lanes] = out * post[
                     3 - i, pl.ds(r0, HALF), lanes
                 ].astype(F32)
             return carry
 
-        lax.fori_loop(0, TILES, tile, 0)
+        lax.fori_loop(0, TILES, tile, 0, unroll=True)
 
     backward_conv(0)
     post_halo = remote(
@@ -489,16 +526,16 @@
     post_halo.start()
     started.append(post_halo)
 
-    f_core.wait_recv()
-    fsum[...] = fpart[core] + fcore[...]
-    f_all = []
-    for i in range(1, CHIPS):
+    own_sum = fpart[quad]
+    for k in range(1, QUAD):
+        slot = lax.rem(quad + QUAD - k, QUAD)
+        here = fcore.at[slot]
+        remote(here, here, fg_s.at[k], fg_r.at[k], (quads[k - 1], me)).wait_recv()
+        own_sum = own_sum + fcore[slot]
+    fsum[...] = own_sum
+    for k in range(1, RINGS):
         copy = remote(
-            fsum,
-            fall.at[chip],
-            fg_s.at[i],
-            fg_r.at[i],
-            (2 * lax.rem(chip + i, CHIPS) + core, me),
+            fsum, fall.at[ring], fg_s.at[3 + k], fg_r.at[3 + k], (along[k - 1], me)
         )
         copy.start()
         started.append(copy)
@@ -532,7 +569,7 @@
                 ).astype(BF16)
             return carry
 
-        lax.fori_loop(0, TILES, tile, 0)
+        lax.fori_loop(0, TILES, tile, 0, unroll=True)
 
     short_back(0)
     short_back(1)
@@ -540,28 +577,43 @@
     store_g.start()
 
     total = fsum[...]
-    for i in range(1, CHIPS):
-        slot = lax.rem(chip + CHIPS - i, CHIPS)
-        remote(fsum, fall.at[slot], fg_s.at[i], fg_r.at[i], sibling).wait_recv()
+    for k in range(1, RINGS):
+        slot = lax.rem(ring + RINGS - k, RINGS)
+        here = fall.at[slot]
+        remote(here, here, fg_s.at[3 + k], fg_r.at[3 + k], (along[k - 1], me)).wait_recv()
         total = total + fall[slot]
-    fout[core] = total * ((N_CTX * ROWS * 16) ** -0.5)
-    f_out = remote(fout.at[core], fout.at[core], fg_s.at[16], fg_r.at[16], sibling)
-    f_out.start()
-    started.append(f_out)
+    fout[quad] = total * ((N_CTX * ROWS * 16) ** -0.5)
+    for k in range(1, QUAD):
+        here = fout.at[quad]
+        copy = remote(here, here, fg_s.at[10 + k], fg_r.at[10 + k], (quads[k - 1], me))
+        copy.start()
+        started.append(copy)
 
     rs_last(1)
     rs_last(0)
     store_m = pltpu.make_async_copy(out_mixed, mixed, lsem.at[4])
     store_m.start()
-    remote(
-        fout.at[1 - core], fout.at[1 - core], fg_s.at[16], fg_r.at[16], sibling
-    ).wait_recv()
+    for k in range(1, QUAD):
+        here = fout.at[lax.rem(quad + QUAD - k, QUAD)]
+        remote(here, here, fg_s.at[10 + k], fg_r.at[10 + k], (quads[k - 1], me)).wait_recv()
     filt[...] = fout[...].reshape(GROUPS, HALF)
 
     for copy in started:
         copy.wait_send()
     store_g.wait()
     store_m.wait()
+
+
+def publish(mixed, fgrads, filt, out_mixed, out_fgrads, out_filt, sem):
+    copies = [
+        pltpu.make_async_copy(fgrads, out_fgrads, sem.at[0]),
+        pltpu.make_async_copy(mixed, out_mixed, sem.at[1]),
+        pltpu.make_async_copy(filt, out_filt, sem.at[2]),
+    ]
+    for copy in copies:
+        copy.start()
+    for copy in copies:
+        copy.wait()
 
 
 def on_device(features, short_filter, long_filter, out_weight, out_cotangent):
@@ -574,7 +626,8 @@
         pltpu.VMEM((ROWS + HALF, CHAN), BF16),
         pltpu.VMEM((ROWS, CHAN), F32),
         pltpu.VMEM((ROWS, CHAN), BF16),
-        pltpu.VMEM((GROUPS * HALF, 2 * HALF), BF16),
+        pltpu.VMEM((GROUPS * STEP, 2 * HALF), BF16),
+        pltpu.VMEM((GROUPS * STEP, 2 * HALF), BF16),
         pltpu.VMEM((GROUPS, 2 * HALF), F32),
         pltpu.VMEM((GROUPS, 2 * HALF), F32),
         pltpu.VMEM((N_TP, ROWS, OUT), BF16),
@@ -591,12 +644,14 @@
         pltpu.VMEM((2, QR, OUT), BF16),
         pltpu.VMEM((ROWS + HALF, CHAN), BF16),
         pltpu.VMEM((3, ROWS + 8, CHAN), F32),
-        pltpu.VMEM((GROUPS, 2 * HALF), F32),
-        pltpu.VMEM((2, GROUPS // 2, HALF), F32),
-        pltpu.VMEM((GROUPS // 2, HALF), F32),
-        pltpu.VMEM((GROUPS // 2, HALF), F32),
-        pltpu.VMEM((CHIPS, GROUPS // 2, HALF), F32),
-        pltpu.VMEM((2, GROUPS // 2, HALF), F32),
+        pltpu.VMEM((GROUPS * STEP, HALF), F32),
+        pltpu.VMEM((GROUPS * STEP, HALF), F32),
+        pltpu.VMEM((CHAN, HALF), F32),
+        pltpu.VMEM((QUAD, SHARE, HALF), F32),
+        pltpu.VMEM((QUAD, SHARE, HALF), F32),
+        pltpu.VMEM((SHARE, HALF), F32),
+        pltpu.VMEM((RINGS, SHARE, HALF), F32),
+        pltpu.VMEM((QUAD, SHARE, HALF), F32),
         pltpu.VMEM((ROWS, OUT), BF16),
         pltpu.VMEM((3, ROWS, CHAN), BF16),
         dma((5,)),
@@ -606,16 +661,17 @@
         dma((2, 11)),
         dma((4,)),
         dma((4,)),
-        dma((17,)),
-        dma((17,)),
+        dma((14,)),
+        dma((14,)),
     ]
-    return pl.pallas_call(
+    shapes = (
+        jax.ShapeDtypeStruct((ROWS, OUT), BF16),
+        jax.ShapeDtypeStruct((3, ROWS, CHAN), BF16),
+        jax.ShapeDtypeStruct((GROUPS, HALF), F32),
+    )
+    results = pl.pallas_call(
         kernel,
-        out_shape=(
-            jax.ShapeDtypeStruct((ROWS, OUT), BF16),
-            jax.ShapeDtypeStruct((3, ROWS, CHAN), BF16),
-            jax.ShapeDtypeStruct((GROUPS, HALF), F32),
-        ),
+        out_shape=shapes,
         in_specs=[hbm, vmem, vmem, hbm, hbm],
         out_specs=(hbm, hbm, vmem),
         scratch_shapes=scratch,
@@ -623,6 +679,13 @@
             collective_id=0, has_side_effects=True, vmem_limit_bytes=56 * 2**20
         ),
     )(features, short_filter, long_filter, out_weight, out_cotangent)
+    return pl.pallas_call(
+        publish,
+        out_shape=shapes,
+        in_specs=[vmem] * 3,
+        out_specs=(hbm,) * 3,
+        scratch_shapes=[dma((3,))],
+    )(*results)
 
 
 def solution(mesh):

time: 77.6 us -> 56.7 us (0.73)
  Pallas kernels: 71.8 us -> 55.6 us
  local copies, waits for them, and re-layouts: 4.96 us -> 0 us
    pallas_call x1 -> x2, Pallas kernels: 71.8 us -> 55.6 us  [the longest x1 53 us: on_device(): pl.pallas_call(kernel, out_shape=shapes, in_specs=[hbm, vmem, vmem, hbm,...]
    unnamed x5 -> x0, local copies, waits for them, and re-layouts: 4.96 us -> none
where the time goes in v2:
time: 56.7 us; the launch traced here: 56.3 us
  Pallas kernels  55.6 us (98%)
  between operations  0.64 us (1%)
    pallas_call x1, Pallas kernels, on_device(): pl.pallas_call(kernel, out_shape=shapes, in_specs=[hbm, vmem, vmem, hbm,...  53 us
    pallas_call x1, Pallas kernels, on_device(): pl.pallas_call(publish, out_shape=shapes, in_specs=[vmem] * 3, out_specs=...  2.67 us

profile of v2, /device:TPU:1, one launch (start us, length us, event | category | flops | bytes accessed | tf_op | source)
XLA Modules:
  0.0 56.3 jit_solution(17067490736533834276)
XLA Ops:
  0.6 53.0 %shard_map.76 = (bf16[256,512]{1,0:T(8,128)(2,1)}, bf16[3,256,1024]{2,1,0:T(8,128)(2,1)}, f32[64,128]{1,0:T(8,128)}) custom-call(bf16[3,256,1024]{2,1,0:T(8,128)(2,1)} %feat.1, bf16[3,3,1024]{2,1,0:T(4,128)(2,1)} %sf.1, bf16[64,128]{1,0:T(8,128)(2,1)} %lf.1, bf16[1024,4096]{1,0:T(8,128)(2,1)} %w_hbm.1, bf16[256,512]{1,0:T(8,128)(2,1)} %cot.1), custom_call_target="tpu_custom_call" | custom-call | tf_op jit(solution)/shard_map/pallas_call | solution.py:672
  53.6 2.7 %shard_map.77 = (bf16[256,512]{1,0:T(8,128)(2,1)}, bf16[3,256,1024]{2,1,0:T(8,128)(2,1)}, f32[64,128]{1,0:T(8,128)}) custom-call(bf16[256,512]{1,0:T(8,128)(2,1)} %get-tuple-element.6.mixed, bf16[3,256,1024]{2,1,0:T(8,128)(2,1)} %get-tuple-element.7.fgrads, f32[64,128]{1,0:T(8,128)} %get-tuple-element.8.filt), custom_call_target="tpu_custom_call" | custom-call | tf_op jit(solution)/shard_map/pallas_call | solution.py:682

commit v3 on v2

v3 whole, which is shorter than its diff:
```python
import functools

import jax
import jax.numpy as jnp
from jax import lax
from jax.experimental import pallas as pl
from jax.experimental.pallas import tpu as pltpu
from jax.sharding import PartitionSpec as P

MESH = pl.DeviceIdType.MESH
F32 = jnp.float32
BF16 = jnp.bfloat16
ROWS = 256
HALF = 128
CHAN = 1024
OUT = 512
N_TP = 8
N_CTX = 32
GROUPS = 64
QR = (48, 32)
PR = (HALF - QR[0], HALF - QR[1])
QM = max(QR)
PM = max(PR)
TILES = CHAN // 128
PER = 8
QUAD = 4
RINGS = N_CTX // QUAD
SHARE = GROUPS // QUAD
STEP = 16
SPAN = HALF + STEP
STEPS = HALF // STEP


def dot(a, b, dims=((1,), (0,))):
    return lax.dot_general(a, b, (dims, ((), ())), preferred_element_type=F32)


def kernel(
    feat,
    sf,
    lf,
    w_hbm,
    cot,
    mixed,
    fgrads,
    filt,
    feats,
    post,
    gated,
    long_out,
    mixer,
    toep_a,
    toep_b,
    vec_a,
    vec_b,
    gath,
    w,
    psum_p,
    psum_q,
    in_up,
    in_own_dn,
    in_own_up,
    in_x,
    in_q,
    in_q_up,
    in_q_own_dn,
    in_q_own_up,
    d_long,
    d_post,
    corr_lo,
    corr_hi,
    d_acc,
    fpart,
    fcore,
    fsum,
    fall,
    fout,
    out_mixed,
    out_grads,
    lsem,
    ag_s,
    ag_r,
    rs_s,
    rs_r,
    halo_s,
    halo_r,
    fg_s,
    fg_r,
    far,
):
    ctx = lax.axis_index("ctx")
    me = lax.axis_index("tp")
    core = lax.rem(ctx, 2)
    quad = lax.rem(ctx, QUAD)
    ring = ctx // QUAD
    corner = ctx - quad
    xl = me // 4
    yl = lax.rem(me, 4)
    step = 1 + 2 * core
    back = 3 - 2 * core
    y_up = lax.rem(yl + step, 4)
    y_dn = lax.rem(yl + back, 4)
    y_op = lax.rem(yl + 2, 4)
    own_base = xl * 4
    x_base = 4 - xl * 4
    up = own_base + y_up
    dn = own_base + y_dn
    op = own_base + y_op
    xo = x_base + yl
    xup = x_base + y_up
    xdn = x_base + y_dn
    xop = x_base + y_op
    nxt = lax.rem(ctx + 1, N_CTX)
    prv = lax.rem(ctx + N_CTX - 1, N_CTX)

    load_f = pltpu.make_async_copy(feat, feats.at[:, pl.ds(16, ROWS), :], lsem.at[0])
    load_w = pltpu.make_async_copy(w_hbm, w, lsem.at[1])
    load_c = pltpu.make_async_copy(cot, gath.at[me], lsem.at[2])
    load_f.start()
    load_w.start()
    load_c.start()

    first = ctx == 0
    final = ctx == N_CTX - 1
    barrier = pltpu.get_barrier_semaphore()

    def greet(sem, dev):
        pl.semaphore_signal(sem, inc=1, device_id=dev, device_id_type=MESH)

    across = core * nxt + (1 - core) * prv
    quads = [corner + lax.rem(quad + k, QUAD) for k in range(1, QUAD)]
    along = [lax.rem(ring + k, RINGS) * QUAD + quad for k in range(1, RINGS)]
    for near in [(ctx, xo), (ctx, up), (ctx, dn)] + [(dev, me) for dev in quads]:
        greet(barrier, near)

    @pl.when(jnp.logical_not(first | final))
    def _():
        greet(barrier, (across, me))

    for k in range(1, RINGS):

        @pl.when(ring + k < RINGS)
        def _(k=k):
            greet(barrier, (along[k - 1], me))

    rows_i = lax.broadcasted_iota(jnp.int32, (HALF, 2 * HALF), 0)
    cols_i = lax.broadcasted_iota(jnp.int32, (HALF, 2 * HALF), 1)
    flip = (cols_i == HALF - rows_i).astype(BF16)
    keep = (cols_i == rows_i).astype(BF16)
    vec_a[...] = dot(lf[...], flip)
    vec_b[...] = dot(lf[...], keep)

    def build(vec, toep):
        def group(g, carry):
            row = jnp.broadcast_to(vec[pl.ds(g, 1), :], (STEP, 2 * HALF))
            there = pl.ds(pl.multiple_of(g * STEP, STEP), STEP)
            toep[there, :] = pltpu.roll(row, 0, 1, stride=1, stride_axis=0).astype(BF16)
            return carry

        lax.fori_loop(0, GROUPS, group, 0, unroll=8)

    build(vec_a, toep_a)
    ends = jnp.where(first | final, 0, 1)
    pl.semaphore_wait(barrier, 6 + ends + ring)

    started = []

    def remote(src, dst, send, recv, dev):
        return pltpu.make_async_remote_copy(
            src_ref=src,
            dst_ref=dst,
            send_sem=send,
            recv_sem=recv,
            device_id=dev,
            device_id_type=MESH,
        )

    QS, PS = 0, 1

    def part_rows(half, part):
        if part == QS:
            return pl.ds(half * HALF, QR[half])
        return pl.ds(half * HALF + QR[half], PR[half])

    def ag_view(slot, half, part):
        return gath.at[slot, part_rows(half, part), :]

    def ag_send(n, half, slot, part, dev, src=None):
        there = ag_view(slot, half, part)
        copy = remote(
            there if src is None else src,
            there,
            ag_s.at[half, n],
            ag_r.at[half, n],
            (ctx, dev),
        )
        copy.start()
        started.append(copy)

    def ag_wait(n, half, slot, part):
        there = ag_view(slot, half, part)
        remote(there, there, ag_s.at[half, n], ag_r.at[half, n], (ctx, xo)).wait_recv()

    def cot_view(half, part):
        return cot.at[part_rows(half, part), :]

    def own_p(half):
        ag_send(0, half, me, PS, xo, cot_view(half, PS))

    def own_q(half):
        ag_send(2, half, me, QS, up, cot_view(half, QS))
        ag_send(3, half, me, QS, dn, cot_view(half, QS))

    def own_r(half):
        ag_send(1, half, me, QS, xo, cot_view(half, QS))
        ag_send(4, half, me, PS, up, cot_view(half, PS))
        ag_send(5, half, me, PS, dn, cot_view(half, PS))

    def pass_q_dn(half):
        ag_wait(2, half, dn, QS)
        ag_send(8, half, dn, QS, up)
        ag_send(9, half, dn, QS, xo)

    def pass_q_up(half):
        ag_wait(3, half, up, QS)
        ag_send(10, half, up, QS, xo)

    def pass_p(half):
        ag_wait(0, half, xo, PS)
        ag_send(6, half, xo, PS, up)
        ag_send(7, half, xo, PS, dn)

    def pass_dn(half):
        ag_wait(4, half, dn, PS)
        ag_send(11, half, dn, PS, up)

    def pass_op(half):
        ag_wait(8, half, op, QS)
        ag_send(12, half, op, QS, xo)

    def pass_xdn(half):
        ag_wait(6, half, xdn, PS)
        ag_send(13, half, xdn, PS, up)

    def short_conv(half):
        r0 = half * HALF

        def tile(c, carry):
            lanes = pl.ds(pl.multiple_of(c * 128, 128), 128)
            kept = []
            for i in range(3):
                ext = feats[i, pl.ds(r0, HALF + 16), lanes].astype(F32)
                taps = sf[i, :, lanes].astype(F32)
                value = (
                    taps[0:1] * ext[16 : 16 + HALF]
                    + taps[1:2] * ext[15 : 15 + HALF]
                    + taps[2:3] * ext[14 : 14 + HALF]
                ).astype(BF16)
                post[i, pl.ds(r0, HALF), lanes] = value
                kept.append(value.astype(F32))
            gated[pl.ds(HALF + r0, HALF), lanes] = (kept[1] * kept[2]).astype(BF16)
            return carry

        lax.fori_loop(0, TILES, tile, 0, unroll=True)

    lane_group = lax.broadcasted_iota(jnp.int32, (STEP, 128), 1) // 16

    def long_conv(toep, source, r0, c, lanes):
        block = toep[pl.ds(pl.multiple_of(c * HALF, HALF), HALF), 0:SPAN]
        window = jnp.concatenate(
            [source[pl.ds(r0 + STEP * a, SPAN), lanes] for a in range(STEPS)], axis=1
        )
        whole = dot(block, window)
        outs = []
        for a in range(STEPS):
            cols = slice(a * 128, (a + 1) * 128)
            out = whole[0:STEP, cols]
            for q in range(1, PER):
                out = jnp.where(lane_group == q, whole[q * STEP : (q + 1) * STEP, cols], out)
            outs.append(out)
        return jnp.concatenate(outs, axis=0)

    def forward_conv(half):
        r0 = half * HALF

        def tile(c, carry):
            lanes = pl.ds(pl.multiple_of(c * 128, 128), 128)
            out = long_conv(toep_a, gated, r0, c, lanes)
            long_out[pl.ds(r0, HALF), lanes] = out
            mixer[pl.ds(r0, HALF), lanes] = (
                post[0, pl.ds(r0, HALF), lanes].astype(F32) * out
            ).astype(BF16)
            return carry

        lax.fori_loop(0, TILES, tile, 0, unroll=True)

    def project(half, side, place, owner):
        cols = pl.ds(pl.multiple_of(owner * OUT, OUT), OUT)
        part = dot(mixer[pl.ds(half * HALF, HALF), :], w[:, cols]).astype(BF16)
        psum_q[half, side, place, 0 : QR[half]] = part[0 : QR[half]]
        psum_p[half, place, side, 0 : PR[half]] = part[QR[half] : HALF]

    def rs_copy(n, half, src, dst, dev):
        return remote(src, dst, rs_s.at[half, n], rs_r.at[half, n], (ctx, dev))

    def rs_all(half):
        p = pl.ds(0, PR[half])
        q = pl.ds(0, QR[half])

        def raw_q(n, place):
            return rs_copy(n, half, psum_q.at[half, 1, place, q], in_q.at[half, place, q], xo)

        copies = [
            rs_copy(0, half, psum_p.at[half, 3, :, p], in_up.at[half, :, p], up),
            rs_copy(1, half, psum_p.at[half, 2, :, p], in_own_up.at[half, :, p], dn),
            raw_q(2, 3),
            raw_q(3, 2),
            raw_q(4, 1),
            raw_q(5, 0),
            rs_copy(6, half, psum_p.at[half, 1, :, p], in_own_dn.at[half, :, p], up),
            rs_copy(7, half, psum_q.at[half, 0, 3, q], in_q_up.at[half, q], up),
            rs_copy(8, half, psum_q.at[half, 0, 2, q], in_q_own_up.at[half, q], dn),
            rs_copy(9, half, psum_q.at[half, 0, 1, q], in_q_own_dn.at[half, q], up),
            rs_copy(10, half, psum_p.at[half, 0, 1, p], in_x.at[half, p], xo),
        ]
        return copies

    rs = [rs_all(0), rs_all(1)]

    def rs_start(half, n):
        rs[half][n].start()
        started.append(rs[half][n])

    def project_far(half):
        project(half, 1, 3, xop)
        project(half, 0, 3, op)
        rs_start(half, 2)
        rs_start(half, 0)

    def project_dn(half):
        project(half, 1, 2, xdn)
        project(half, 0, 2, dn)
        rs_start(half, 3)
        rs_start(half, 1)

    def project_up(half):
        project(half, 1, 1, xup)
        project(half, 1, 0, xo)
        rs_start(half, 4)
        rs_start(half, 5)
        project(half, 0, 1, up)
        project(half, 0, 0, me)

    def add(a, *others):
        total = a.astype(F32)
        for other in others:
            total = total + other.astype(F32)
        return total.astype(BF16)

    def q_rows(ref, half, *place):
        return ref[(half, *place, pl.ds(0, QR[half]))]

    def p_rows(ref, half, *place):
        return ref[(half, *place, pl.ds(0, PR[half]))]

    def rs_a(half):
        rs[half][2].wait_recv()
        psum_q[half, 0, 3, 0 : QR[half]] = add(q_rows(psum_q, half, 0, 3), q_rows(in_q, half, 3))
        rs_start(half, 7)

    def rs_b(half):
        rs[half][0].wait_recv()
        for side in (0, 1):
            psum_p[half, 1, side, 0 : PR[half]] = add(
                p_rows(psum_p, half, 1, side), p_rows(in_up, half, side)
            )
        rs_start(half, 6)

    def rs_c(half):
        rs[half][3].wait_recv()
        psum_q[half, 0, 2, 0 : QR[half]] = add(q_rows(psum_q, half, 0, 2), q_rows(in_q, half, 2))
        rs_start(half, 8)

    def rs_d(half):
        rs[half][4].wait_recv()
        rs[half][7].wait_recv()
        psum_q[half, 0, 1, 0 : QR[half]] = add(
            q_rows(psum_q, half, 0, 1), q_rows(in_q, half, 1), q_rows(in_q_up, half)
        )
        rs_start(half, 9)

    def rs_e(half):
        rs[half][1].wait_recv()
        rs[half][6].wait_recv()
        psum_p[half, 0, 1, 0 : PR[half]] = add(
            p_rows(psum_p, half, 0, 1), p_rows(in_own_dn, half, 1), p_rows(in_own_up, half, 1)
        )
        rs_start(half, 10)

    def rs_last(half):
        rs[half][5].wait_recv()
        rs[half][8].wait_recv()
        rs[half][9].wait_recv()
        out_mixed[part_rows(half, QS), :] = add(
            q_rows(psum_q, half, 0, 0),
            q_rows(in_q, half, 0),
            q_rows(in_q_own_dn, half),
            q_rows(in_q_own_up, half),
        )
        rs[half][10].wait_recv()
        out_mixed[part_rows(half, PS), :] = add(
            p_rows(psum_p, half, 0, 0),
            p_rows(in_own_dn, half, 0),
            p_rows(in_own_up, half, 0),
            p_rows(in_x, half),
        )

    def d_mixer(slots, start, last):
        for c in range(CHAN // 256):
            chans = pl.ds(c * 256, 256)
            total = None if start else d_acc[chans, :]
            for s in slots:
                cols = pl.ds(pl.multiple_of(s * OUT, OUT), OUT)
                part = dot(w[chans, cols], gath[s], ((1,), (1,)))
                total = part if total is None else total + part
            if not last:
                d_acc[chans, :] = total
                continue
            grad = total.T.astype(BF16).astype(F32)
            d_post[0, pl.ds(0, ROWS), chans] = grad * long_out[:, chans]
            d_long[pl.ds(0, ROWS), chans] = (grad * post[0, :, chans].astype(F32)).astype(BF16)

    def ag_wait_both(*which):
        for half in (0, 1):
            for n, slot, part in which:
                ag_wait(n, half, slot, part)

    wide_group = lax.rem(lax.broadcasted_iota(jnp.int32, (STEP, 2 * CHAN), 1), 128) // 16

    def correlate():
        for c in range(TILES):
            lanes = pl.ds(c * 128, 128)
            grads = jnp.concatenate(
                [d_long[pl.ds(STEP * a, STEP), lanes] for a in range(2 * STEPS)], axis=1
            )
            stack = jnp.concatenate(
                [jnp.where(wide_group == q, grads, jnp.zeros_like(grads)) for q in range(PER)],
                axis=0,
            )
            window = jnp.concatenate(
                [gated[pl.ds(STEP * a, SPAN), lanes] for a in range(2 * STEPS)], axis=1
            )
            whole = dot(stack, window, ((1,), (1,)))
            there = pl.ds(c * HALF, HALF)
            corr_lo[there, :] = whole[:, 0:128]
            corr_hi[there, 0:STEP] = whole[:, 128:SPAN]

    def corr_row(b):
        rows = pl.ds(b, GROUPS, stride=STEP)
        return jnp.concatenate([corr_lo[rows, :], corr_hi[rows, :]], axis=1)

    def filter_sums():
        taps_sum = corr_row(0)
        for b in range(1, STEP):
            taps_sum = taps_sum + pltpu.roll(corr_row(b), 2 * HALF - b, 1)
        lane_i = lax.broadcasted_iota(jnp.int32, (GROUPS, 2 * HALF), 1)
        taps_sum = jnp.where((lane_i >= 1) & (lane_i <= HALF), taps_sum, 0.0)
        fpart[...] = lax.dot_general(
            taps_sum,
            (cols_i == HALF - rows_i).astype(F32),
            (((1,), (1,)), ((), ())),
            preferred_element_type=F32,
            precision=lax.Precision.HIGHEST,
        ).reshape(QUAD, SHARE, HALF)

    def quad_copy(src, dst, k, base):
        return remote(src, dst, fg_s.at[base + k], fg_r.at[base + k], (quads[k - 1], me))

    def filter_first():
        for k in range(1, QUAD):
            copy = quad_copy(fpart.at[lax.rem(quad + k, QUAD)], fcore.at[quad], k, 0)
            copy.start()
            started.append(copy)

    def filter_second():
        own_sum = fpart[quad]
        for k in range(1, QUAD):
            slot = lax.rem(quad + QUAD - k, QUAD)
            here = fcore.at[slot]
            quad_copy(here, here, k, 0).wait_recv()
            own_sum = own_sum + fcore[slot]
        fsum[...] = own_sum

        @pl.when(ring < RINGS - 1)
        def _():
            pl.semaphore_wait(far, RINGS - 1 - ring)

        for k in range(1, RINGS):
            copy = remote(
                fsum, fall.at[ring], fg_s.at[3 + k], fg_r.at[3 + k], (along[k - 1], me)
            )
            copy.start()
            started.append(copy)

    def filter_third():
        total = fsum[...]
        for k in range(1, RINGS):
            slot = lax.rem(ring + RINGS - k, RINGS)
            here = fall.at[slot]
            remote(here, here, fg_s.at[3 + k], fg_r.at[3 + k], (along[k - 1], me)).wait_recv()
            total = total + fall[slot]
        fout[quad] = total * ((N_CTX * ROWS * 16) ** -0.5)
        for k in range(1, QUAD):
            here = fout.at[quad]
            copy = quad_copy(here, here, k, 10)
            copy.start()
            started.append(copy)

    def filter_last():
        for k in range(1, QUAD):
            here = fout.at[lax.rem(quad + QUAD - k, QUAD)]
            quad_copy(here, here, k, 10).wait_recv()
        filt[...] = fout[...].reshape(GROUPS, HALF)

    def backward_conv(half):
        r0 = half * HALF

        def tile(c, carry):
            lanes = pl.ds(pl.multiple_of(c * 128, 128), 128)
            out = long_conv(toep_b, d_long, r0, c, lanes)
            for i in (1, 2):
                d_post[i, pl.ds(r0, HALF), lanes] = out * post[
                    3 - i, pl.ds(r0, HALF), lanes
                ].astype(F32)
            return carry

        lax.fori_loop(0, TILES, tile, 0, unroll=True)

    def short_back(half):
        r0 = half * HALF

        def tile(c, carry):
            lanes = pl.ds(pl.multiple_of(c * 128, 128), 128)
            for i in range(3):
                ext = d_post[i, pl.ds(r0, HALF + 8), lanes]
                taps = sf[i, :, lanes].astype(F32)
                out_grads[i, pl.ds(r0, HALF), lanes] = (
                    taps[0:1] * ext[0:HALF]
                    + taps[1:2] * ext[1 : 1 + HALF]
                    + taps[2:3] * ext[2 : 2 + HALF]
                ).astype(BF16)
            return carry

        lax.fori_loop(0, TILES, tile, 0, unroll=True)

    def halo(n, src, dst, dev):
        return remote(src, dst, halo_s.at[n], halo_r.at[n], (dev, me))

    feat_halo = halo(0, feat.at[:, pl.ds(ROWS - 16, 16), :], feats.at[:, pl.ds(0, 16), :], nxt)
    gated_halo = halo(1, gated.at[pl.ds(2 * HALF, HALF), :], gated.at[pl.ds(0, HALF), :], nxt)
    long_halo = halo(2, d_long.at[pl.ds(0, HALF), :], d_long.at[pl.ds(2 * HALF, HALF), :], prv)
    post_halo = halo(3, d_post.at[:, pl.ds(0, 8), :], d_post.at[:, pl.ds(ROWS, 8), :], prv)

    def halo_start(copy, none):
        @pl.when(jnp.logical_not(none))
        def _():
            copy.start()

    def halo_wait(copy, none, ref, shape):
        @pl.when(none)
        def _():
            ref[...] = jnp.zeros(shape, ref.dtype)

        @pl.when(jnp.logical_not(none))
        def _():
            copy.wait_recv()

    halo_start(feat_halo, final)
    own_p(0)
    own_q(0)
    for k in range(1, RINGS):

        @pl.when(ring - k >= 0)
        def _(k=k):
            greet(far, (lax.rem(ctx + N_CTX - QUAD * k, N_CTX), me))

    own_q(1)
    own_p(1)
    own_r(1)
    pass_q_dn(1)
    own_r(0)
    build(vec_b, toep_b)
    pass_q_dn(0)
    load_f.wait()
    short_conv(1)
    halo_start(gated_halo, final)
    pass_p(0)
    pass_p(1)
    load_w.wait()
    load_c.wait()
    ag_wait_both((1, xo, QS))
    d_mixer((me, xo), True, False)
    pass_dn(0)
    pass_q_up(1)
    halo_wait(feat_halo, first, feats.at[:, pl.ds(0, 16), :], (3, 16, CHAN))
    short_conv(0)
    pass_dn(1)
    pass_q_up(0)
    ag_wait_both((5, up, PS))
    d_mixer((dn, up), False, False)
    pass_op(1)
    pass_xdn(0)
    pass_xdn(1)
    pass_op(0)
    forward_conv(1)
    project_far(1)
    project_dn(1)
    ag_wait_both((7, xup, PS), (9, xdn, QS), (10, xup, QS))
    d_mixer((xup, xdn), False, False)
    halo_wait(gated_halo, first, gated.at[pl.ds(0, HALF), :], (HALF, CHAN))
    forward_conv(0)
    project_far(0)
    ag_wait_both((11, op, PS))
    d_mixer((op,), False, False)
    project_dn(0)
    ag_wait_both((12, xop, QS), (13, xop, PS))
    d_mixer((xop,), False, True)
    halo_start(long_halo, first)
    correlate()
    filter_sums()
    filter_first()
    project_up(1)
    rs_b(1)
    project_up(0)
    rs_a(1)
    rs_b(0)
    filter_second()
    backward_conv(0)
    halo_start(post_halo, first)
    rs_a(0)
    rs_e(1)
    rs_c(0)
    rs_c(1)
    rs_d(1)
    halo_wait(long_halo, final, d_long.at[pl.ds(2 * HALF, HALF), :], (HALF, CHAN))
    backward_conv(1)
    rs_e(0)
    filter_third()
    rs_d(0)
    rs_last(1)
    halo_wait(post_halo, final, d_post.at[:, pl.ds(ROWS, 8), :], (3, 8, CHAN))
    short_back(0)
    short_back(1)
    store_g = pltpu.make_async_copy(out_grads, fgrads, lsem.at[3])
    store_g.start()
    rs_last(0)
    store_m = pltpu.make_async_copy(out_mixed, mixed, lsem.at[4])
    store_m.start()
    filter_last()

    for copy in started:
        copy.wait_send()

    @pl.when(jnp.logical_not(final))
    def _():
        feat_halo.wait_send()
        gated_halo.wait_send()

    @pl.when(jnp.logical_not(first))
    def _():
        long_halo.wait_send()
        post_halo.wait_send()

    store_g.wait()
    store_m.wait()


def publish(mixed, fgrads, filt, out_mixed, out_fgrads, out_filt, hold_m, hold_g, hold_f, sem):
    pairs = [(fgrads.at[i], hold_g.at[i], out_fgrads.at[i]) for i in range(3)]
    pairs += [(mixed, hold_m, out_mixed), (filt, hold_f, out_filt)]
    loads = [
        pltpu.make_async_copy(src, mid, sem.at[n]) for n, (src, mid, _) in enumerate(pairs)
    ]
    stores = [
        pltpu.make_async_copy(mid, dst, sem.at[5 + n]) for n, (_, mid, dst) in enumerate(pairs)
    ]
    for load in loads:
        load.start()
    for load, store in zip(loads, stores):
        load.wait()
        store.start()
    for store in stores:
        store.wait()


def on_device(features, short_filter, long_filter, out_weight, out_cotangent):
    hbm = pl.BlockSpec(memory_space=pl.ANY)
    vmem = pl.BlockSpec(memory_space=pltpu.VMEM)
    dma = pltpu.SemaphoreType.DMA
    scratch = [
        pltpu.VMEM((3, ROWS + 16, CHAN), BF16),
        pltpu.VMEM((3, ROWS, CHAN), BF16),
        pltpu.VMEM((ROWS + HALF, CHAN), BF16),
        pltpu.VMEM((ROWS, CHAN), F32),
        pltpu.VMEM((ROWS, CHAN), BF16),
        pltpu.VMEM((GROUPS * STEP, 2 * HALF), BF16),
        pltpu.VMEM((GROUPS * STEP, 2 * HALF), BF16),
        pltpu.VMEM((GROUPS, 2 * HALF), F32),
        pltpu.VMEM((GROUPS, 2 * HALF), F32),
        pltpu.VMEM((N_TP, ROWS, OUT), BF16),
        pltpu.VMEM((CHAN, N_TP * OUT), BF16),
        pltpu.VMEM((2, 4, 2, PM, OUT), BF16),
        pltpu.VMEM((2, 2, 4, QM, OUT), BF16),
        pltpu.VMEM((2, 2, PM, OUT), BF16),
        pltpu.VMEM((2, 2, PM, OUT), BF16),
        pltpu.VMEM((2, 2, PM, OUT), BF16),
        pltpu.VMEM((2, PM, OUT), BF16),
        pltpu.VMEM((2, 4, QM, OUT), BF16),
        pltpu.VMEM((2, QM, OUT), BF16),
        pltpu.VMEM((2, QM, OUT), BF16),
        pltpu.VMEM((2, QM, OUT), BF16),
        pltpu.VMEM((ROWS + HALF, CHAN), BF16),
        pltpu.VMEM((3, ROWS + 8, CHAN), F32),
        pltpu.VMEM((GROUPS * STEP, HALF), F32),
        pltpu.VMEM((GROUPS * STEP, HALF), F32),
        pltpu.VMEM((CHAN, ROWS), F32),
        pltpu.VMEM((QUAD, SHARE, HALF), F32),
        pltpu.VMEM((QUAD, SHARE, HALF), F32),
        pltpu.VMEM((SHARE, HALF), F32),
        pltpu.VMEM((RINGS, SHARE, HALF), F32),
        pltpu.VMEM((QUAD, SHARE, HALF), F32),
        pltpu.VMEM((ROWS, OUT), BF16),
        pltpu.VMEM((3, ROWS, CHAN), BF16),
        dma((5,)),
        dma((2, 14)),
        dma((2, 14)),
        dma((2, 11)),
        dma((2, 11)),
        dma((4,)),
        dma((4,)),
        dma((14,)),
        dma((14,)),
        pltpu.SemaphoreType.REGULAR,
    ]
    shapes = (
        jax.ShapeDtypeStruct((ROWS, OUT), BF16),
        jax.ShapeDtypeStruct((3, ROWS, CHAN), BF16),
        jax.ShapeDtypeStruct((GROUPS, HALF), F32),
    )
    results = pl.pallas_call(
        kernel,
        out_shape=shapes,
        in_specs=[hbm, vmem, vmem, hbm, hbm],
        out_specs=(hbm, hbm, vmem),
        scratch_shapes=scratch,
        compiler_params=pltpu.CompilerParams(
            collective_id=0, has_side_effects=True, vmem_limit_bytes=56 * 2**20
        ),
    )(features, short_filter, long_filter, out_weight, out_cotangent)
    return pl.pallas_call(
        publish,
        out_shape=shapes,
        in_specs=[hbm] * 3,
        out_specs=(hbm,) * 3,
        scratch_shapes=[
            pltpu.VMEM((ROWS, OUT), BF16),
            pltpu.VMEM((3, ROWS, CHAN), BF16),
            pltpu.VMEM((GROUPS, HALF), F32),
            dma((10,)),
        ],
    )(*results)


def solution(mesh):
    placed = (
        P(None, "ctx", "tp"),
        P(None, None, "tp"),
        P("tp", None),
        P("tp", None),
        P("ctx", "tp"),
    )
    return jax.shard_map(
        on_device,
        mesh=mesh,
        in_specs=placed,
        out_specs=(P("ctx", "tp"), P(None, "ctx", "tp"), P("tp", None)),
        check_vma=False,
    )
```

time: 56.7 us -> 53.1 us (0.937)
  Pallas kernels: 55.6 us -> 52.3 us
    pallas_call x1, Pallas kernels: 53 us -> 49.9 us  [on_device(): pl.pallas_call(kernel, out_shape=shapes, in_specs=[hbm, vmem, vmem, hbm,...]
where the time goes in v3:
time: 53.1 us; the launch traced here: 52.9 us
  Pallas kernels  52.3 us (98%)
  between operations  0.64 us (1%)
    pallas_call x1, Pallas kernels, on_device(): pl.pallas_call(kernel, out_shape=shapes, in_specs=[hbm, vmem, vmem, hbm,...  49.9 us
    pallas_call x1, Pallas kernels, on_device(): pl.pallas_call(publish, out_shape=shapes, in_specs=[hbm] * 3, out_specs=(...  2.35 us

profile of v3, /device:TPU:1, one launch (start us, length us, event | category | flops | bytes accessed | tf_op | source)
XLA Modules:
  0.0 52.9 jit_solution(17124909046979158246)
XLA Ops:
  0.6 49.9 %shard_map.76 = (bf16[256,512]{1,0:T(8,128)(2,1)}, bf16[3,256,1024]{2,1,0:T(8,128)(2,1)}, f32[64,128]{1,0:T(8,128)}) custom-call(bf16[3,256,1024]{2,1,0:T(8,128)(2,1)} %feat.1, bf16[3,3,1024]{2,1,0:T(4,128)(2,1)} %sf.1, bf16[64,128]{1,0:T(8,128)(2,1)} %lf.1, bf16[1024,4096]{1,0:T(8,128)(2,1)} %w_hbm.1, bf16[256,512]{1,0:T(8,128)(2,1)} %cot.1), custom_call_target="tpu_custom_call" | custom-call | tf_op jit(solution)/shard_map/pallas_call | solution.py:750
  50.5 2.4 %shard_map.77 = (bf16[256,512]{1,0:T(8,128)(2,1)}, bf16[3,256,1024]{2,1,0:T(8,128)(2,1)}, f32[64,128]{1,0:T(8,128)}) custom-call(bf16[256,512]{1,0:T(8,128)(2,1)} %get-tuple-element.6.mixed, bf16[3,256,1024]{2,1,0:T(8,128)(2,1)} %get-tuple-element.7.fgrads, f32[64,128]{1,0:T(8,128)} %get-tuple-element.8.filt), custom_call_target="tpu_custom_call" | custom-call | tf_op jit(solution)/shard_map/pallas_call | solution.py:760

commit v4 on v3

--- a/solution.py
+++ b/solution.py
@@ -630,22 +630,22 @@
     filter_sums()
     filter_first()
     project_up(1)
+    project_up(0)
     rs_b(1)
-    project_up(0)
+    backward_conv(0)
+    halo_start(post_halo, first)
+    filter_second()
     rs_a(1)
     rs_b(0)
-    filter_second()
-    backward_conv(0)
-    halo_start(post_halo, first)
     rs_a(0)
     rs_e(1)
+    rs_c(1)
     rs_c(0)
-    rs_c(1)
     rs_d(1)
+    filter_third()
     halo_wait(long_halo, final, d_long.at[pl.ds(2 * HALF, HALF), :], (HALF, CHAN))
     backward_conv(1)
     rs_e(0)
-    filter_third()
     rs_d(0)
     rs_last(1)
     halo_wait(post_halo, final, d_post.at[:, pl.ds(ROWS, 8), :], (3, 8, CHAN))

time: 53.1 us -> 53.4 us (level)
  no operation moved by 1% of the time
where the time goes in v4:
time: 53.4 us; the launch traced here: 53.3 us
  Pallas kernels  52.6 us (99%)
  between operations  0.64 us (1%)
    pallas_call x1, Pallas kernels, on_device(): pl.pallas_call(kernel, out_shape=shapes, in_specs=[hbm, vmem, vmem, hbm,...  50.3 us
    pallas_call x1, Pallas kernels, on_device(): pl.pallas_call(publish, out_shape=shapes, in_specs=[hbm] * 3, out_specs=(...  2.35 us

profile of v4, /device:TPU:1, one launch (start us, length us, event | category | flops | bytes accessed | tf_op | source)
XLA Modules:
  0.0 53.3 jit_solution(14413677819281876826)
XLA Ops:
  0.6 50.3 %shard_map.76 = (bf16[256,512]{1,0:T(8,128)(2,1)}, bf16[3,256,1024]{2,1,0:T(8,128)(2,1)}, f32[64,128]{1,0:T(8,128)}) custom-call(bf16[3,256,1024]{2,1,0:T(8,128)(2,1)} %feat.1, bf16[3,3,1024]{2,1,0:T(4,128)(2,1)} %sf.1, bf16[64,128]{1,0:T(8,128)(2,1)} %lf.1, bf16[1024,4096]{1,0:T(8,128)(2,1)} %w_hbm.1, bf16[256,512]{1,0:T(8,128)(2,1)} %cot.1), custom_call_target="tpu_custom_call" | custom-call | tf_op jit(solution)/shard_map/pallas_call | solution.py:750
  50.9 2.4 %shard_map.77 = (bf16[256,512]{1,0:T(8,128)(2,1)}, bf16[3,256,1024]{2,1,0:T(8,128)(2,1)}, f32[64,128]{1,0:T(8,128)}) custom-call(bf16[256,512]{1,0:T(8,128)(2,1)} %get-tuple-element.6.mixed, bf16[3,256,1024]{2,1,0:T(8,128)(2,1)} %get-tuple-element.7.fgrads, f32[64,128]{1,0:T(8,128)} %get-tuple-element.8.filt), custom_call_target="tpu_custom_call" | custom-call | tf_op jit(solution)/shard_map/pallas_call | solution.py:760
